TPU v7x, 32 devices: a whole 2x2x4 slice. The times are simulated.
32 devices in a mesh: ctx: 2 (over y), fsdp: 16 (over z, x, core).
Axes of the slice: x: 2, y: 2, z: 4, core: 2. Of those that a mesh axis runs over, the one named last changes fastest.
Arguments:
- tokens: bfloat16 [2, 16, 1536, 1024], P(None, 'fsdp', 'ctx'), may hold values from -6 to 6
- encoded: bfloat16 [2, 16, 1024, 1024], P(None, 'fsdp', 'ctx'), may hold values from -6 to 6
- cotangent: bfloat16 [2, 16, 1536, 1024], P(None, 'fsdp', 'ctx'), may hold values from -6 to 6
- order: int32 [2, 16, 1536], P(None, 'fsdp'), may hold values from 0 to 1535, as said below
- target_lengths: int32 [2, 16, 4], P(None, 'fsdp'), may hold values from 1 to 1152, as said below
- source_lengths: int32 [2, 16, 4], P(None, 'fsdp'), may hold values from 1 to 512, 1024 in all within a row
- self_project: bfloat16 [1024, 3072], P('fsdp'), may hold values from -0.25 to 0.25
- self_output: bfloat16 [1024, 1024], P('fsdp'), may hold values from -0.75 to 0.75
- cross_query: bfloat16 [1024, 1024], P('fsdp'), may hold values from -0.25 to 0.25
- cross_source: bfloat16 [1024, 2048], P('fsdp'), may hold values from -0.25 to 0.25
- cross_output: bfloat16 [1024, 1024], P('fsdp'), may hold values from -0.75 to 0.75
- feed_in: bfloat16 [1024, 4096], P('fsdp'), may hold values from -0.1875 to 0.1875
- feed_out: bfloat16 [4096, 1024], P('fsdp'), may hold values from -0.09375 to 0.09375
- norm_gain: bfloat16 [3, 1024], P(None, 'fsdp'), may hold values from 0.5 to 1.5
- norm_bias: bfloat16 [3, 1024], P(None, 'fsdp'), may hold values from -2 to 2
Outputs:
- output: bfloat16 [2, 16, 1536, 1024], P(None, 'fsdp', 'ctx')
- grad_tokens: bfloat16 [2, 16, 1536, 1024], P(None, 'fsdp', 'ctx')
- grad_encoded: bfloat16 [2, 16, 1024, 1024], P(None, 'fsdp', 'ctx')
- grad_self_project: float32 [1024, 3072], P('fsdp')
- grad_self_output: float32 [1024, 1024], P('fsdp')
- grad_cross_query: float32 [1024, 1024], P('fsdp')
- grad_cross_source: float32 [1024, 2048], P('fsdp')
- grad_cross_output: float32 [1024, 1024], P('fsdp')
- grad_feed_in: float32 [1024, 4096], P('fsdp')
- grad_feed_out: float32 [4096, 1024], P('fsdp')
- grad_norm_gain: float32 [3, 1024], P(None, 'fsdp')
- grad_norm_bias: float32 [2, 1024], P(None, 'fsdp')
- grad_feed_norm_bias: float32 [1024], P('fsdp')
Inputs may be any that keep to these rules, and one draw needn't show every extreme that they name: Within a pack the slots form blocks of 384 in a row; each pair of blocks 2i, 2i + 1 holds, in increasing order, the positions of one of the first 1536 / 768 position blocks and of one of the later ones; each position once. `target_lengths`: A pack's lengths sum to 1536; its first document has exactly 1152 positions. `source_lengths`: A pack's lengths sum to 1024; source document k belongs to target document k.
All inputs are finite; a program needn't handle non-finite values.
Results may differ from a plain program's by a relative error of at most 0.029.
Values may be sent and summed in bfloat16 or wider, within the bound.
No kernel may reach another device: no remote copies, remote signals or barrier semaphores. Data moves between devices by JAX's collectives and lax.ppermute only.
A program may use at most 232 MiB of HBM per device.

v0:
```python
import functools
import math

import jax
import jax.numpy as jnp
from jax import lax
from jax.experimental import pallas as pl
from jax.experimental.pallas import tpu as pltpu
from jax.sharding import PartitionSpec as P

HEAD = 64


MASKED = -1e30


def as_sent(x):

    def short(part):
        return part.astype(jnp.bfloat16) if part.dtype == jnp.float32 else part

    return jax.tree.map(short, x)


def norm_apply(values, gain, bias):
    mean = jnp.mean(values, axis=-1, keepdims=True)
    centred = values - mean
    spread = jnp.mean(centred * centred, axis=-1, keepdims=True)
    return centred * lax.rsqrt(spread + 1e-05) * gain + bias


def gelu_exact(values):
    return jax.nn.gelu(values, approximate=False)


def docs_of(places, lengths):
    ends = jnp.cumsum(lengths)
    return jnp.sum((places[:, None] >= ends[None, :]).astype(jnp.int32), axis=1)


def split_heads(values):
    return values.reshape(values.shape[0], -1, HEAD)


def block_scores(query, pairs, allowed, start, count):
    model = query.shape[1]
    block = lax.dynamic_slice_in_dim(pairs, start, count, 0)
    scores = jnp.einsum(
        "qhd,khd->hqk",
        split_heads(query),
        split_heads(block[:, :model]),
        preferred_element_type=jnp.float32,
    )
    scores = jnp.where(allowed(start, count)[None], scores * HEAD ** (-0.5), MASKED)
    return (scores, block)


def log_mass(query, pairs, allowed, width):
    rows, model = query.shape
    heads = model // HEAD

    def step(index, carry):
        peak, total = carry
        scores, _ = block_scores(query, pairs, allowed, index * width, width)
        new_peak = jnp.maximum(peak, jnp.max(scores, axis=2))
        total = total * jnp.exp(peak - new_peak) + jnp.sum(
            jnp.exp(scores - new_peak[:, :, None]), axis=2
        )
        return (new_peak, total)

    begin = (jnp.full((heads, rows), MASKED, jnp.float32), jnp.zeros((heads, rows), jnp.float32))
    peak, total = lax.fori_loop(0, pairs.shape[0] // width, step, begin)
    return peak + jnp.log(total)


def attend_forward(query, pairs, allowed, width, log_total):
    rows, model = query.shape

    def step(index, mixed):
        scores, block = block_scores(query, pairs, allowed, index * width, width)
        probs = jnp.exp(scores - log_total[:, :, None]).astype(jnp.bfloat16)
        return mixed + jnp.einsum(
            "hqk,khd->qhd", probs, split_heads(block[:, model:]), preferred_element_type=jnp.float32
        )

    mixed = lax.fori_loop(
        0, pairs.shape[0] // width, step, jnp.zeros((rows, model // HEAD, HEAD), jnp.float32)
    )
    return mixed.reshape(rows, model).astype(jnp.bfloat16)


def score_grads(query, pairs, allowed, grad_mixed, log_total, start, count):
    model = query.shape[1]
    scores, block = block_scores(query, pairs, allowed, start, count)
    probs = jnp.exp(scores - log_total[:, :, None])
    grad_probs = jnp.einsum(
        "qhd,khd->hqk",
        split_heads(grad_mixed),
        split_heads(block[:, model:]),
        preferred_element_type=jnp.float32,
    )
    return (probs, grad_probs, block)


def attend_delta(query, pairs, allowed, grad_mixed, log_total, width):
    rows, model = query.shape

    def step(index, delta):
        probs, grad_probs, _ = score_grads(
            query, pairs, allowed, grad_mixed, log_total, index * width, width
        )
        return delta + jnp.sum(probs * grad_probs, axis=2)

    return lax.fori_loop(
        0, pairs.shape[0] // width, step, jnp.zeros((model // HEAD, rows), jnp.float32)
    )


def attend_query_grad(query, pairs, allowed, grad_mixed, log_total, delta, width):
    rows, model = query.shape

    def step(index, grad):
        probs, grad_probs, block = score_grads(
            query, pairs, allowed, grad_mixed, log_total, index * width, width
        )
        grad_scores = (probs * (grad_probs - delta[:, :, None])).astype(jnp.bfloat16)
        return grad + jnp.einsum(
            "hqk,khd->qhd",
            grad_scores,
            split_heads(block[:, :model]),
            preferred_element_type=jnp.float32,
        )

    grad = lax.fori_loop(
        0, pairs.shape[0] // width, step, jnp.zeros((rows, model // HEAD, HEAD), jnp.float32)
    )
    return (grad.reshape(rows, model) * HEAD ** (-0.5)).astype(jnp.bfloat16)


def key_terms(query, pairs, allowed, grad_mixed, log_total, delta, width, count):
    model = query.shape[1]
    step_width = math.gcd(count, width)

    def step(index, terms):
        probs, grad_probs, _ = score_grads(
            query, pairs, allowed, grad_mixed, log_total, index * step_width, step_width
        )
        grad_scores = (probs * (grad_probs - delta[:, :, None])).astype(jnp.bfloat16)
        grad_keys = jnp.einsum(
            "hqk,qhd->khd", grad_scores, split_heads(query), preferred_element_type=jnp.float32
        ) * HEAD ** (-0.5)
        grad_values = jnp.einsum(
            "hqk,qhd->khd",
            probs.astype(jnp.bfloat16),
            split_heads(grad_mixed),
            preferred_element_type=jnp.float32,
        )
        piece = jnp.concatenate(
            [grad_keys.reshape(step_width, model), grad_values.reshape(step_width, model)], axis=1
        )
        return lax.dynamic_update_slice_in_dim(terms, piece, index * step_width, 0)

    return lax.fori_loop(0, count // step_width, step, jnp.zeros((count, 2 * model), jnp.float32))


def body(
    tokens,
    encoded,
    cotangent,
    order,
    target_lengths,
    source_lengths,
    self_project,
    self_output,
    cross_query,
    cross_source,
    cross_output,
    feed_in,
    feed_out,
    norm_gain,
    norm_bias,
):
    micro = tokens.shape[0]
    rows = tokens.shape[2]
    model = tokens.shape[3]
    source_rows = encoded.shape[2]
    place = lax.axis_index("ctx")
    group = lax.axis_size("ctx")
    pack_total = rows * group
    source_total = source_rows * group
    self_width = math.gcd(pack_total, 512)
    cross_width = math.gcd(source_total, 512)
    results = []
    grad_values_all = []
    grad_encoded_all = []
    totals = ()
    for index in range(micro):
        attention_part = (
            lax.all_gather(self_project, "fsdp", axis=0, tiled=True),
            lax.all_gather(self_output, "fsdp", axis=0, tiled=True),
            lax.all_gather(cross_query, "fsdp", axis=0, tiled=True),
            lax.all_gather(cross_source, "fsdp", axis=0, tiled=True),
            lax.all_gather(cross_output, "fsdp", axis=0, tiled=True),
            lax.all_gather(norm_gain, "fsdp", axis=1, tiled=True),
            lax.all_gather(norm_bias, "fsdp", axis=1, tiled=True),
        )
        feed_part = (
            lax.all_gather(feed_in, "fsdp", axis=0, tiled=True),
            lax.all_gather(feed_out, "fsdp", axis=0, tiled=True),
        )
        weights = tuple(attention_part) + tuple(feed_part)
        (
            self_in_full,
            self_out_full,
            cross_query_full,
            cross_source_full,
            cross_out_full,
            gain_full,
            bias_full,
            feed_in_full,
            feed_out_full,
        ) = weights
        gains = gain_full.astype(jnp.float32)
        biases = bias_full.astype(jnp.float32)
        values = tokens[index, 0].astype(jnp.float32)
        source = encoded[index, 0]
        grad_out = cotangent[index, 0]
        places = order[index, 0]
        target_docs = docs_of(places, target_lengths[index, 0])
        query_places = lax.dynamic_slice_in_dim(places, place * rows, rows)
        query_docs = lax.dynamic_slice_in_dim(target_docs, place * rows, rows)
        source_docs = docs_of(jnp.arange(source_total, dtype=jnp.int32), source_lengths[index, 0])

        def self_allowed(start, count):
            key_docs = lax.dynamic_slice_in_dim(target_docs, start, count)
            key_places = lax.dynamic_slice_in_dim(places, start, count)
            return (query_docs[:, None] == key_docs[None, :]) & (
                key_places[None, :] <= query_places[:, None]
            )

        def cross_allowed(start, count):
            return (
                query_docs[:, None] == lax.dynamic_slice_in_dim(source_docs, start, count)[None, :]
            )

        first = norm_apply(values, gains[0], biases[0]).astype(jnp.bfloat16)
        query = jnp.dot(first, self_in_full[:, :model], preferred_element_type=jnp.float32).astype(
            jnp.bfloat16
        )
        local_pairs = jnp.dot(
            first, self_in_full[:, model:], preferred_element_type=jnp.float32
        ).astype(jnp.bfloat16)
        self_pairs = lax.all_gather(local_pairs, "ctx", axis=0, tiled=True)
        self_total = log_mass(query, self_pairs, self_allowed, self_width)
        self_mixed = attend_forward(query, self_pairs, self_allowed, self_width, self_total)
        after_self = values + jnp.dot(self_mixed, self_out_full, preferred_element_type=jnp.float32)
        second = norm_apply(after_self, gains[1], biases[1]).astype(jnp.bfloat16)
        cross_queries = jnp.dot(
            second, cross_query_full, preferred_element_type=jnp.float32
        ).astype(jnp.bfloat16)
        cross_local = jnp.dot(source, cross_source_full, preferred_element_type=jnp.float32).astype(
            jnp.bfloat16
        )
        cross_pairs = lax.all_gather(cross_local, "ctx", axis=0, tiled=True)
        cross_total = log_mass(cross_queries, cross_pairs, cross_allowed, cross_width)
        cross_mixed = attend_forward(
            cross_queries, cross_pairs, cross_allowed, cross_width, cross_total
        )
        after_cross = after_self + jnp.dot(
            cross_mixed, cross_out_full, preferred_element_type=jnp.float32
        )
        third = norm_apply(after_cross, gains[2], biases[2]).astype(jnp.bfloat16)
        hidden = jnp.dot(third, feed_in_full, preferred_element_type=jnp.float32)
        active = gelu_exact(hidden).astype(jnp.bfloat16)
        result = (
            after_cross + jnp.dot(active, feed_out_full, preferred_element_type=jnp.float32)
        ).astype(jnp.bfloat16)
        grad_feed_out = jnp.einsum(
            "rf,rd->fd", active, grad_out, preferred_element_type=jnp.float32
        )
        grad_active = jnp.einsum(
            "rd,fd->rf", grad_out, feed_out_full, preferred_element_type=jnp.float32
        ).astype(jnp.bfloat16)
        _, gelu_pull = jax.vjp(gelu_exact, hidden)
        grad_hidden = gelu_pull(grad_active.astype(jnp.float32))[0].astype(jnp.bfloat16)
        grad_feed_in = jnp.einsum(
            "rd,rf->df", third, grad_hidden, preferred_element_type=jnp.float32
        )
        grad_third = jnp.einsum(
            "rf,df->rd", grad_hidden, feed_in_full, preferred_element_type=jnp.float32
        )
        _, norm_pull = jax.vjp(norm_apply, after_cross, gains[2], biases[2])
        norm_part, gain_two, bias_two = norm_pull(grad_third)
        grad_after_cross = grad_out.astype(jnp.float32) + norm_part
        cross_branch = grad_after_cross.astype(jnp.bfloat16)
        grad_cross_output = jnp.einsum(
            "rd,re->de", cross_mixed, cross_branch, preferred_element_type=jnp.float32
        )
        grad_cross_mixed = jnp.einsum(
            "re,de->rd", cross_branch, cross_out_full, preferred_element_type=jnp.float32
        ).astype(jnp.bfloat16)
        cross_delta = attend_delta(
            cross_queries, cross_pairs, cross_allowed, grad_cross_mixed, cross_total, cross_width
        )
        grad_cross_queries = attend_query_grad(
            cross_queries,
            cross_pairs,
            cross_allowed,
            grad_cross_mixed,
            cross_total,
            cross_delta,
            cross_width,
        )
        grad_source = lax.psum_scatter(
            key_terms(
                cross_queries,
                cross_pairs,
                cross_allowed,
                grad_cross_mixed,
                cross_total,
                cross_delta,
                cross_width,
                source_rows * lax.axis_size("ctx"),
            ).astype(jnp.bfloat16),
            "ctx",
            scatter_dimension=0,
            tiled=True,
        )
        grad_cross_source = jnp.einsum(
            "sd,se->de", source, grad_source, preferred_element_type=jnp.float32
        )
        grad_encoded = jnp.einsum(
            "se,de->sd", grad_source, cross_source_full, preferred_element_type=jnp.float32
        ).astype(jnp.bfloat16)
        grad_cross_query = jnp.einsum(
            "rd,re->de", second, grad_cross_queries, preferred_element_type=jnp.float32
        )
        grad_second = jnp.einsum(
            "re,de->rd", grad_cross_queries, cross_query_full, preferred_element_type=jnp.float32
        )
        _, norm_pull = jax.vjp(norm_apply, after_self, gains[1], biases[1])
        norm_part, gain_one, bias_one = norm_pull(grad_second)
        grad_after_self = grad_after_cross + norm_part
        self_branch = grad_after_self.astype(jnp.bfloat16)
        grad_self_output = jnp.einsum(
            "rd,re->de", self_mixed, self_branch, preferred_element_type=jnp.float32
        )
        grad_self_mixed = jnp.einsum(
            "re,de->rd", self_branch, self_out_full, preferred_element_type=jnp.float32
        ).astype(jnp.bfloat16)
        self_delta = attend_delta(
            query, self_pairs, self_allowed, grad_self_mixed, self_total, self_width
        )
        grad_query = attend_query_grad(
            query, self_pairs, self_allowed, grad_self_mixed, self_total, self_delta, self_width
        )
        grad_pairs = lax.psum_scatter(
            key_terms(
                query,
                self_pairs,
                self_allowed,
                grad_self_mixed,
                self_total,
                self_delta,
                self_width,
                rows * lax.axis_size("ctx"),
            ).astype(jnp.bfloat16),
            "ctx",
            scatter_dimension=0,
            tiled=True,
        )
        grad_projected = jnp.concatenate([grad_query, grad_pairs], axis=1)
        grad_self_project = jnp.einsum(
            "rd,re->de", first, grad_projected, preferred_element_type=jnp.float32
        )
        grad_first = jnp.einsum(
            "re,de->rd", grad_projected, self_in_full, preferred_element_type=jnp.float32
        )
        _, norm_pull = jax.vjp(norm_apply, values, gains[0], biases[0])
        norm_part, gain_zero, bias_zero = norm_pull(grad_first)
        grad_values = (grad_after_self + norm_part).astype(jnp.bfloat16)
        grads = (
            grad_self_project,
            grad_self_output,
            grad_cross_query,
            grad_cross_source,
            grad_cross_output,
            grad_feed_in,
            grad_feed_out,
            jnp.stack([gain_zero, gain_one, gain_two]),
            jnp.stack([bias_zero, bias_one, bias_two]),
        )
        result, grad_values, grad_encoded, grads = (result, grad_values, grad_encoded, grads)
        totals = (
            grads
            if index == 0
            else tuple((jnp.add(left, right) for left, right in zip(totals, grads)))
        )
        results.append(result)
        grad_values_all.append(grad_values)
        grad_encoded_all.append(grad_encoded)
    shares = (
        lax.psum_scatter(
            totals[0].astype(jnp.bfloat16), "fsdp", scatter_dimension=0, tiled=True
        ).astype(jnp.float32),
        lax.psum_scatter(
            totals[1].astype(jnp.bfloat16), "fsdp", scatter_dimension=0, tiled=True
        ).astype(jnp.float32),
        lax.psum_scatter(
            totals[2].astype(jnp.bfloat16), "fsdp", scatter_dimension=0, tiled=True
        ).astype(jnp.float32),
        lax.psum_scatter(
            totals[3].astype(jnp.bfloat16), "fsdp", scatter_dimension=0, tiled=True
        ).astype(jnp.float32),
        lax.psum_scatter(
            totals[4].astype(jnp.bfloat16), "fsdp", scatter_dimension=0, tiled=True
        ).astype(jnp.float32),
        lax.psum_scatter(
            totals[5].astype(jnp.bfloat16), "fsdp", scatter_dimension=0, tiled=True
        ).astype(jnp.float32),
        lax.psum_scatter(
            totals[6].astype(jnp.bfloat16), "fsdp", scatter_dimension=0, tiled=True
        ).astype(jnp.float32),
        lax.psum_scatter(
            totals[7].astype(jnp.bfloat16), "fsdp", scatter_dimension=1, tiled=True
        ).astype(jnp.float32),
        lax.psum_scatter(
            totals[8].astype(jnp.bfloat16), "fsdp", scatter_dimension=1, tiled=True
        ).astype(jnp.float32),
    )
    totals = tuple(
        jax.tree.map(lambda part: part.astype(jnp.float32), lax.psum(as_sent(tuple(shares)), "ctx"))
    )
    output = jnp.stack(results)[:, None]
    grad_tokens = jnp.stack(grad_values_all)[:, None]
    grad_source_rows = jnp.stack(grad_encoded_all)[:, None]
    return (
        output,
        grad_tokens,
        grad_source_rows,
        totals[0],
        totals[1],
        totals[2],
        totals[3],
        totals[4],
        totals[5],
        totals[6],
        totals[7],
        totals[8][:2],
        totals[8][2],
    )


BIG = 1e30
SCALE2 = HEAD ** (-0.5) * math.log2(math.e)
NT = (((1,), (1,)), ((), ()))
TN = (((0,), (0,)), ((), ()))
NN = (((1,), (0,)), ((), ()))


def dot(left, right, dims=NN):
    return lax.dot_general(left, right, dims, preferred_element_type=jnp.float32)


def lanes(rows):
    return lax.broadcasted_iota(jnp.int32, (rows, 128), 1)


def parts(x):
    hi = x.astype(jnp.bfloat16)
    rest = x - hi.astype(jnp.float32)
    mid = rest.astype(jnp.bfloat16)
    lo = (rest - mid.astype(jnp.float32)).astype(jnp.bfloat16)
    return (hi, mid, lo)


def spread(x, base):
    hi, mid, lo = parts(x)
    lane = lanes(x.shape[0]) % HEAD
    return jnp.where(lane == 4, hi, jnp.where(lane == 5, mid, jnp.where(lane == 6, lo, base)))


def two_heads(ref, own, other):
    left = lanes(own.shape[0]) < HEAD
    ref[0] = jnp.where(left, own, other)
    ref[1] = jnp.where(left, other, own)


def tail_masked(scores, rows):
    width = scores.shape[1] - rows
    row = lax.broadcasted_iota(jnp.int32, (rows, rows), 0)
    column = lax.broadcasted_iota(jnp.int32, (rows, rows), 1)
    tail = jnp.where(column > row, -BIG, scores[:, width:])
    return tail if width == 0 else jnp.concatenate([scores[:, :width], tail], axis=1)


def attend_kernel(plan, q_ref, k_ref, v_ref, qd_ref, kd_ref, out_ref, extra_ref, keys, values):
    two_heads(keys, k_ref[...], kd_ref[...])
    two_heads(values, v_ref[...], jnp.ones_like(v_ref))

    def scores_of(item):
        q0, q1, k0, k1, diagonal = item
        left = lanes(q1 - q0) < HEAD
        q, qd = (q_ref[q0:q1], qd_ref[q0:q1])
        pair = [dot(jnp.where(left == (h == 0), q, qd), keys[h, k0:k1], NT) for h in range(2)]
        return [tail_masked(s, q1 - q0) for s in pair] if diagonal else pair

    following = scores_of(plan[0])
    for index, (q0, q1, k0, k1, _) in enumerate(plan):
        scores = following
        following = scores_of(plan[index + 1]) if index + 1 < len(plan) else None
        left = lanes(q1 - q0) < HEAD
        mixed, tops = ([], [])
        for h in range(2):
            top = jnp.max(scores[h], axis=1, keepdims=True)
            probs = jnp.exp2((scores[h] - top) * SCALE2).astype(jnp.bfloat16)
            mixed.append(dot(probs, values[h, k0:k1]))
            tops.append(top)
        mass = jnp.where(left, mixed[1], mixed[0])
        numer = jnp.where(left, mixed[0], mixed[1])
        out_ref[q0:q1] = (numer / pltpu.roll(mass, HEAD, 1)).astype(jnp.bfloat16)
        top = jnp.where(left, tops[1], tops[0])
        extra_ref[q0:q1] = spread(-(top + HEAD**0.5 * jnp.log(mass)), qd_ref[q0:q1])


def attend_back_kernel(
    plan,
    q_ref,
    k_ref,
    v_ref,
    extra_ref,
    kd_ref,
    out_ref,
    g_ref,
    *refs,
):
    *outs, keys, values, queries, grads, g_t, q_t, dk_t, dv_t = refs
    if len(outs) == 1:
        dq_ref, dk_ref, dv_ref = (outs[0].at[i] for i in range(3))
    else:
        dq_ref, dk_ref, dv_ref = (outs[0], outs[1].at[0], outs[1].at[1])
    two_heads(keys, k_ref[...], kd_ref[...])
    two_heads(values, v_ref[...], jnp.ones_like(v_ref))
    two_heads(queries, q_ref[...], extra_ref[...])
    square = (128, 128)
    row, column = (lax.broadcasted_iota(jnp.int32, square, axis) < HEAD for axis in (0, 1))
    across = jnp.where(row != column, 1.0, 0.0).astype(jnp.bfloat16)
    g = g_ref[...]
    terms = parts(g.astype(jnp.float32) * out_ref[...].astype(jnp.float32))
    delta = sum(dot(term, across) for term in terms)
    two_heads(grads, g, spread(-delta, jnp.zeros_like(g)))
    g_t[...] = g.T
    q_t[...] = q_ref[...].T
    dk_t[...] = jnp.zeros_like(dk_t)
    dv_t[...] = jnp.zeros_like(dv_t)
    for q0, q1, k0, k1, diagonal in plan:
        left = lanes(q1 - q0) < HEAD
        pair = []
        for h in range(2):
            s = dot(queries[h, q0:q1], keys[h, k0:k1], NT)
            s = tail_masked(s, q1 - q0) if diagonal else s
            pair.append((s, dot(grads[h, q0:q1], values[h, k0:k1], NT)))
        dqs = []
        for h, (s, grad_probs) in enumerate(pair):
            probs = jnp.exp2(s * SCALE2)
            ds = (probs * grad_probs).astype(jnp.bfloat16)
            head = slice(h * HEAD, h * HEAD + HEAD)
            dv_t[head, k0:k1] += dot(g_t[head, q0:q1], probs.astype(jnp.bfloat16))
            dk_t[head, k0:k1] += dot(q_t[head, q0:q1], ds)
            dqs.append(dot(ds, k_ref[k0:k1]))
        dq_ref[q0:q1] = (jnp.where(left, dqs[0], dqs[1]) * HEAD ** (-0.5)).astype(jnp.bfloat16)
    dk_ref[...] = (dk_t[...].T * HEAD ** (-0.5)).astype(jnp.bfloat16)
    dv_ref[...] = dv_t[...].T.astype(jnp.bfloat16)


def pair_of_heads(rows):
    return pl.BlockSpec((rows, 128), lambda i: (0, i))


def all_of(rows):
    return pl.BlockSpec((rows, 128), lambda i: (0, 0))


def small_cost():
    return pl.CostEstimate(flops=1 << 10, bytes_accessed=1 << 10, transcendentals=0)


def attend(plan, q, k, v, qd, kd):
    nq, nk, model = (q.shape[0], k.shape[0], q.shape[1])
    shape = jax.ShapeDtypeStruct((nq, model), jnp.bfloat16)
    return pl.pallas_call(
        functools.partial(attend_kernel, plan),
        grid=(model // 128,),
        in_specs=[pair_of_heads(n) for n in (nq, nk, nk)] + [all_of(nq), all_of(nk)],
        out_specs=[pair_of_heads(nq)] * 2,
        out_shape=[shape] * 2,
        scratch_shapes=[pltpu.VMEM((2, nk, 128), jnp.bfloat16)] * 2,
        compiler_params=pltpu.CompilerParams(vmem_limit_bytes=58 * 2**20),
        cost_estimate=small_cost(),
    )(q, k, v, qd, kd)


def stacked(count, rows):
    return pl.BlockSpec((count, rows, 128), lambda i: (0, 0, i))


def attend_back(plan, q, k, v, extra, kd, out, g, together):
    nq, nk, model = (q.shape[0], k.shape[0], q.shape[1])
    if together:
        specs, shapes = ([stacked(3, nq)], [(3, nq, model)])
    else:
        specs, shapes = ([pair_of_heads(nq), stacked(2, nk)], [(nq, model), (2, nk, model)])
    outs = pl.pallas_call(
        functools.partial(attend_back_kernel, plan),
        grid=(model // 128,),
        in_specs=[pair_of_heads(n) for n in (nq, nk, nk, nq)]
        + [all_of(nk)]
        + [pair_of_heads(nq)] * 2,
        out_specs=specs,
        out_shape=[jax.ShapeDtypeStruct(shape, jnp.bfloat16) for shape in shapes],
        scratch_shapes=[pltpu.VMEM((2, nk, 128), jnp.bfloat16)] * 2
        + [pltpu.VMEM((2, nq, 128), jnp.bfloat16)] * 2
        + [pltpu.VMEM((128, nq), jnp.bfloat16)] * 2
        + [pltpu.VMEM((128, nk), jnp.float32)] * 2,
        compiler_params=pltpu.CompilerParams(vmem_limit_bytes=58 * 2**20),
        cost_estimate=small_cost(),
    )(q, k, v, extra, kd, out, g)
    return outs[0] if together else outs


def self_plan(first, total, tile):
    return [
        (start, start + tile, low, start + tile, True)
        for low, high in ((0, first), (first, total))
        for start in range(low, high, tile)
    ]


def cross_plan(first, total, reach, source, tile):
    return [
        (start, start + tile, 0, reach if start < first else source, False)
        for start in range(0, total, tile)
    ]


def query_marks(docs):
    lane = jnp.arange(128) % HEAD
    return jnp.where(docs[:, None] == lane[None, :], BIG, 0.0).astype(jnp.bfloat16)


def key_marks(docs, count):
    lane = (jnp.arange(128) % HEAD)[None, :]
    other = jnp.where(docs[:, None] == lane, 0.0, -1.0)
    return jnp.where(lane < count, other, jnp.where(lane < 7, 1.0, 0.0)).astype(jnp.bfloat16)


MODEL = 1024
TILE = 512


def wide(values):
    return values.astype(jnp.float32)


def short(values):
    return values.astype(jnp.bfloat16)


def gathered(ref):
    return ref[...].reshape(-1, ref.shape[-1])


def once(shape, index):
    return pl.BlockSpec(shape, index, pipeline_mode=pl.Buffered(1))


def weight_at(slot):
    return once((16, 64, MODEL), lambda *_: (0, slot, 0))


def norm_rows():
    return once((8, MODEL), lambda *_: (0, 0))


def by_rows(count, width=MODEL):
    return pl.BlockSpec((count, width), lambda i, *_: (i, 0))


def found_rows(count):
    return pl.BlockSpec((count, MODEL), lambda i, held, *_: (held[i], 0))


def kept_or_sent(rows):
    return [once((rows, MODEL), lambda *_: (0, 0)) for _ in range(2)]


def store_found(held, width, own_ref, away_ref, value):
    spot = held[pl.program_id(0)]
    rows = pl.ds(pl.multiple_of(lax.rem(spot, 2) * width, width), width)

    @pl.when(spot < 2)
    def _():
        own_ref[rows] = value

    @pl.when(spot >= 2)
    def _():
        away_ref[rows] = value


def sums_out():
    return pl.BlockSpec((8, MODEL), lambda *_: (0, 0))


def struct(shape, kind):
    return jax.ShapeDtypeStruct(shape, kind)


def spread_of(values):
    mean = jnp.mean(values, axis=-1, keepdims=True)
    centred = values - mean
    scale = lax.rsqrt(jnp.mean(centred * centred, axis=-1, keepdims=True) + 1e-05)
    return (centred * scale, scale)


def norm_of(values, norm_ref, k):
    hat, _ = spread_of(values)
    return short(hat * norm_ref[k : k + 1] + norm_ref[3 + k : 4 + k])


def norm_back(values, grad, norm_ref, k, sums_ref):
    hat, scale = spread_of(values)
    each = grad * norm_ref[k : k + 1]
    inner = each - jnp.mean(each, axis=-1, keepdims=True)
    inner = inner - hat * jnp.mean(each * hat, axis=-1, keepdims=True)
    sums_ref[0:1] += jnp.sum(grad * hat, axis=0, keepdims=True)
    sums_ref[1:2] += jnp.sum(grad, axis=0, keepdims=True)
    return scale * inner


def call(kernel, grid, in_specs, out_specs, out_shape, scratch=(), prefetch=0):
    return pl.pallas_call(
        kernel,
        grid_spec=pltpu.PrefetchScalarGridSpec(
            num_scalar_prefetch=prefetch,
            grid=grid,
            in_specs=in_specs,
            out_specs=out_specs,
            scratch_shapes=list(scratch),
        ),
        out_shape=out_shape,
        compiler_params=pltpu.CompilerParams(vmem_limit_bytes=58 * 2**20),
        cost_estimate=small_cost(),
    )


def pack_kernel(*refs):
    attention_ref, feed_ref = refs[-2:]
    self_in, self_out, cross_q, cross_s, cross_out, feed_in, feed_out, norms = refs[:-2]
    rows = self_in.shape[0]
    slot = 0
    for ref in (self_in, self_out, cross_q, cross_s, cross_out):
        for start in range(0, ref.shape[1], MODEL):
            attention_ref[slot * rows : (slot + 1) * rows] = ref[:, start : start + MODEL]
            slot += 1
    attention_ref[slot * rows :] = norms[...]
    piece = feed_out.shape[0] // 2
    for lot in range(2):
        for owner in range(16):
            column = (2 * owner + lot) * piece
            slot, spot = (2 * lot + owner // 8, owner % 8 * piece)
            feed_ref[slot * rows : (slot + 1) * rows, spot : spot + piece] = feed_in[
                :, column : column + piece
            ]
    feed_ref[4 * rows : 8 * rows] = feed_out[...]
    feed_ref[8 * rows :] = jnp.zeros_like(norms)


def pack(weights, norms):
    arrays = tuple(weights) + (norms,)
    out = struct((528, MODEL), jnp.bfloat16)
    return call(
        pack_kernel,
        (1,),
        [once(a.shape, lambda i: (0, 0)) for a in arrays],
        [once(out.shape, lambda i: (0, 0))] * 2,
        [out] * 2,
    )(*arrays)


def enter_kernel(held, tokens_ref, norm_ref, wq, wk, wv, first_ref, q_ref, k_ref, v_ref):
    first = norm_of(wide(tokens_ref[...]), norm_ref, 0)
    first_ref[...] = first
    for weight, out in ((wq, q_ref), (wk, k_ref), (wv, v_ref)):
        out[...] = short(dot(first, gathered(weight)))


def enter(held, tokens, norms, weights, width):
    shape = struct(tokens.shape, jnp.bfloat16)
    return call(
        enter_kernel,
        (tokens.shape[0] // width,),
        [found_rows(width), norm_rows()] + [weight_at(i) for i in range(3)],
        [by_rows(width)] * 4,
        [shape] * 4,
        prefetch=1,
    )(held, tokens, norms, weights, weights, weights)


def source_kernel(source_ref, wk, wv, k_ref, v_ref):
    source = source_ref[...]
    k_ref[...] = short(dot(source, gathered(wk)))
    v_ref[...] = short(dot(source, gathered(wv)))


def source_pairs(source, weights, width):
    return call(
        source_kernel,
        (source.shape[0] // width,),
        [by_rows(width), weight_at(5), weight_at(6)],
        [by_rows(width)] * 2,
        [struct(source.shape, jnp.bfloat16)] * 2,
    )(source, weights, weights)


def between_kernel(held, mixed_ref, tokens_ref, norm_ref, wo, wq, after_ref, second_ref, q_ref):
    after = wide(tokens_ref[...]) + dot(mixed_ref[...], gathered(wo))
    after_ref[...] = after
    second = norm_of(after, norm_ref, 1)
    second_ref[...] = second
    q_ref[...] = short(dot(second, gathered(wq)))


def between(held, mixed, tokens, norms, weights, width):
    return call(
        between_kernel,
        (mixed.shape[0] // width,),
        [by_rows(width), found_rows(width), norm_rows(), weight_at(3), weight_at(4)],
        [by_rows(width)] * 3,
        [struct(mixed.shape, kind) for kind in (jnp.float32, jnp.bfloat16, jnp.bfloat16)],
        prefetch=1,
    )(held, mixed, tokens, norms, weights, weights)


def before_feed_kernel(
    held, mixed_ref, base_ref, own_ref, other_ref, norm_ref, wo, after_ref, third_ref, grad_ref
):
    after = base_ref[...] + dot(mixed_ref[...], gathered(wo))
    after_ref[...] = after
    third_ref[...] = norm_of(after, norm_ref, 2)
    own = held[pl.program_id(0)] < 2

    @pl.when(own)
    def _():
        grad_ref[...] = own_ref[...]

    @pl.when(jnp.logical_not(own))
    def _():
        grad_ref[...] = other_ref[...]


def before_feed(held, mixed, base, own, other, norms, weights, width):
    return call(
        before_feed_kernel,
        (mixed.shape[0] // width,),
        [
            by_rows(width),
            by_rows(width),
            pl.BlockSpec((width, MODEL), lambda i, held: (jnp.minimum(held[i], 1), 0)),
            pl.BlockSpec((width, MODEL), lambda i, held: (jnp.maximum(held[i] - 2, 0), 0)),
            norm_rows(),
            weight_at(7),
        ],
        [by_rows(width)] * 3,
        [struct(mixed.shape, kind) for kind in (jnp.float32, jnp.bfloat16, jnp.bfloat16)],
        prefetch=1,
    )(held, mixed, base, own, other, norms, weights)


def gelu_terms(hidden):
    bell = jnp.exp2(hidden * hidden * (-0.5 * math.log2(math.e)))
    t = 1.0 / (1.0 + (0.3275911 / math.sqrt(2.0)) * jnp.abs(hidden))
    series = 1.061405429
    for term in (-1.453152027, 1.421413741, -0.284496736, 0.254829592):
        series = series * t + term
    tail = 0.5 * series * t * bell
    return (jnp.where(hidden < 0, tail, 1.0 - tail), bell * (1.0 / math.sqrt(2.0 * math.pi)))


def deal(place_ref, turned, keep_ref, send_ref, pieces, own_y=True):
    for own in range(2):

        @pl.when(place_ref[0] == own)
        def _(own=own):
            for core, x, y, index, value in pieces:
                rel_x = jnp.bitwise_xor(place_ref[1], x)
                rel_y = jnp.bitwise_xor(place_ref[2], y) if own_y else y
                spot = (rel_y, rel_x) if turned else (rel_x, rel_y)
                ref = keep_ref if core == own else send_ref
                ref[spot + index] = value


def shard_pieces(product, slot, *rest):
    pieces = []
    for owner in range(product.shape[0] // 64):
        for y in range(2):
            start = owner * 64 + y * 32
            index = (owner // 4, slot) + rest
            value = short(product[start : start + 32])
            pieces.append((owner % 2, owner // 2 % 2, y, index, value))
    return pieces


def feed_kernel(
    place_ref,
    third_ref,
    grad_ref,
    win_ref,
    wout_ref,
    out_ref,
    back_ref,
    keep_a,
    send_a,
    keep_b,
    send_b,
    third_t,
    active_ref,
    hidden_ref,
):
    step = pl.program_id(0)

    @pl.when(step == 0)
    def _():
        third_t[...] = third_ref[...].T
        out_ref[...] = jnp.zeros_like(out_ref)
        back_ref[...] = jnp.zeros_like(back_ref)

    win, wout = (gathered(win_ref), gathered(wout_ref))
    rows = third_ref.shape[0]
    lots = [slice(start, start + TILE) for start in range(0, rows, TILE)]

    def enter(lot):
        return (dot(third_ref[lot], win), dot(grad_ref[lot], wout, NT))

    def leave(lot, hidden, grad):
        mass, bell = gelu_terms(hidden)
        active = short(hidden * mass)
        grad = short((mass + hidden * bell) * wide(short(grad)))
        active_ref[lot] = active
        hidden_ref[lot] = grad
        out_ref[lot] += dot(active, wout)
        back_ref[lot] += dot(grad, win, NT)

    ready = enter(lots[0])
    for index, lot in enumerate(lots):
        following = enter(lots[index + 1]) if index + 1 < len(lots) else None
        leave(lot, *ready)
        ready = following
    grad_out = short(dot(active_ref[...], grad_ref[...], TN))
    grad_in = short(dot(third_t[...], hidden_ref[...]))
    turn = lax.rem(step, 4)
    side = pl.ds(pl.multiple_of(lax.rem(turn, 2) * TILE, TILE), TILE)
    pieces = shard_pieces(grad_in, turn // 2, slice(None), side)
    for owner in range(4):
        for y in range(2):
            for half in range(2):
                start = owner * 128 + y * 64 + 32 * half
                value = grad_out[start : start + 32]
                pieces.append((owner % 2, owner // 2, y, (turn, 2 + half), value))

    @pl.when(step < 4)
    def _():
        deal(place_ref, False, keep_a, send_a, pieces)

    @pl.when(step >= 4)
    def _():
        deal(place_ref, True, keep_b, send_b, pieces)


def feed(place, third, grad, weights):
    rows = third.shape[0]
    full = struct((rows, MODEL), jnp.float32)
    buffer = struct((2, 2, 4, 4, 32, MODEL), jnp.bfloat16)
    out, back, *lots = call(
        feed_kernel,
        (8,),
        [
            once((rows, MODEL), lambda t, place: (0, 0)),
            once((rows, MODEL), lambda t, place: (0, 0)),
            pl.BlockSpec((16, 64, TILE), lambda t, place: (0, t // 2, t % 2)),
            pl.BlockSpec((4, 128, MODEL), lambda t, place: (t % 4, 2 + t // 4, 0)),
        ],
        [once((rows, MODEL), lambda t, place: (0, 0))] * 2
        + [once(buffer.shape, lambda t, place: (0, 0, 0, 0, 0, 0))] * 4,
        [full, full] + [buffer] * 4,
        scratch=[
            pltpu.VMEM((MODEL, rows), jnp.bfloat16),
            pltpu.VMEM((rows, TILE), jnp.bfloat16),
            pltpu.VMEM((rows, TILE), jnp.bfloat16),
        ],
        prefetch=1,
    )(place, third, grad, weights, weights)
    return out, back, lots[:2], lots[2:]


def clear(*refs):
    @pl.when(pl.program_id(0) == 0)
    def _():
        for ref in refs:
            ref[...] = jnp.zeros_like(ref)


def add_product(total_ref, left, right):
    total_ref[...] += dot(left, right, TN)


def at_end(store):
    pl.when(pl.program_id(0) == pl.num_programs(0) - 1)(store)


def buffer_of(slots):
    return struct((2, 2, 4, slots, 32, MODEL), jnp.bfloat16)


def slots_at(slots):
    return once((2, 2, 4, slots, 32, MODEL), lambda *_: (0,) * 6)


def after_feed_kernel(
    held,
    place,
    after_ref,
    out_ref,
    back_ref,
    grad_ref,
    cross_ref,
    norm_ref,
    wo,
    own_ref,
    away_ref,
    total_ref,
    mixed_ref,
    sums_ref,
    keep_ref,
    send_ref,
    weight_ref,
):
    clear(sums_ref, weight_ref)
    after = after_ref[...]
    result = short(after + out_ref[...])
    store_found(held, after.shape[0], own_ref, away_ref, result)
    part = norm_back(after, back_ref[...], norm_ref, 2, sums_ref)
    total = wide(grad_ref[...]) + part
    total_ref[...] = total
    branch = short(total)
    mixed_ref[...] = short(dot(branch, gathered(wo), NT))
    add_product(weight_ref, cross_ref[...], branch)
    at_end(lambda: deal(place, False, keep_ref, send_ref, shard_pieces(weight_ref, 0)))


def after_feed(held, place, after, out, back, grad, mixed, norms, weights, width):
    narrow = struct(after.shape, jnp.bfloat16)
    full = struct(after.shape, jnp.float32)
    return call(
        after_feed_kernel,
        (after.shape[0] // width,),
        [by_rows(width)] * 5 + [norm_rows(), weight_at(7)],
        kept_or_sent(2 * width) + [by_rows(width)] * 2 + [sums_out()] + [slots_at(1)] * 2,
        [struct((2 * width, MODEL), jnp.bfloat16)] * 2
        + [full, narrow, struct((8, MODEL), jnp.float32)]
        + [buffer_of(1)] * 2,
        scratch=[pltpu.VMEM((MODEL, MODEL), jnp.float32)],
        prefetch=2,
    )(held, place, after, out, back, grad, mixed, norms, weights)


def middle_kernel(
    place,
    grad_ref,
    second_ref,
    after_ref,
    base_ref,
    self_ref,
    norm_ref,
    wq,
    wo,
    *refs,
):
    total_ref, mixed_ref, sums_ref, keep_ref, send_ref, weight_q, weight_o = refs
    clear(sums_ref, weight_q, weight_o)
    grad_q = grad_ref[...]
    grad = dot(grad_q, gathered(wq), NT)
    add_product(weight_q, second_ref[...], grad_q)
    total = base_ref[...] + norm_back(after_ref[...], grad, norm_ref, 1, sums_ref)
    total_ref[...] = total
    branch = short(total)
    mixed_ref[...] = short(dot(branch, gathered(wo), NT))
    add_product(weight_o, self_ref[...], branch)

    @at_end
    def _():
        deal(place, False, keep_ref, send_ref, shard_pieces(weight_q, 0))
        deal(place, False, keep_ref, send_ref, shard_pieces(weight_o, 1))


def middle(place, grad, second, after, base, mixed, norms, weights, width):
    narrow = struct(after.shape, jnp.bfloat16)
    return call(
        middle_kernel,
        (after.shape[0] // width,),
        [by_rows(width)] * 5 + [norm_rows(), weight_at(4), weight_at(3)],
        [by_rows(width)] * 2 + [sums_out()] + [slots_at(2)] * 2,
        [struct(after.shape, jnp.float32), narrow, struct((8, MODEL), jnp.float32)]
        + [buffer_of(2)] * 2,
        scratch=[pltpu.VMEM((MODEL, MODEL), jnp.float32)] * 2,
        prefetch=1,
    )(place, grad, second, after, base, mixed, norms, weights, weights)


def project_grad_kernel(place, left_ref, right_ref, keep_ref, send_ref, left_t):
    @pl.when(pl.program_id(1) == 0)
    def _():
        left_t[...] = left_ref[...].T

    product = dot(left_t[...], right_ref[0])
    deal(place, False, keep_ref, send_ref, shard_pieces(product, 0), own_y=False)


def project_grad(place, left, right):
    rows = left.shape[0]
    block = (2, 2, TILE // 256, 1, 32, MODEL)
    return call(
        project_grad_kernel,
        (MODEL // TILE, 3),
        [
            pl.BlockSpec((rows, TILE), lambda t, n, place: (0, t)),
            pl.BlockSpec((1, rows, MODEL), lambda t, n, place: (n, 0, 0)),
        ],
        [pl.BlockSpec(block, lambda t, n, place: (0, 0, t, n, 0, 0))] * 2,
        [buffer_of(3)] * 2,
        scratch=[pltpu.VMEM((TILE, rows), jnp.bfloat16)],
        prefetch=1,
    )(place, left, right)


def finish_kernel(
    held, grads_ref, tokens_ref, base_ref, norm_ref, wq, wk, wv, own_ref, away_ref, sums_ref
):
    clear(sums_ref)
    grad = sum(dot(grads_ref[i], gathered(w), NT) for i, w in enumerate((wq, wk, wv)))
    part = norm_back(wide(tokens_ref[...]), grad, norm_ref, 0, sums_ref)
    result = short(base_ref[...] + part)
    store_found(held, result.shape[0], own_ref, away_ref, result)


def finish(held, grads, tokens, base, norms, weights, width):
    return call(
        finish_kernel,
        (base.shape[0] // width,),
        [
            pl.BlockSpec((3, width, MODEL), lambda i, *_: (0, i, 0)),
            found_rows(width),
            by_rows(width),
            norm_rows(),
        ]
        + [weight_at(i) for i in range(3)],
        kept_or_sent(2 * width) + [sums_out()],
        [struct((2 * width, MODEL), jnp.bfloat16)] * 2 + [struct((8, MODEL), jnp.float32)],
        prefetch=1,
    )(held, grads, tokens, base, norms, weights, weights, weights)


def source_back_kernel(
    place, grads_ref, source_ref, wk, wv, own_ref, away_ref, keep_ref, send_ref, weight_ref
):
    clear(weight_ref)
    source = source_ref[...].T
    for i in range(2):
        weight_ref[i] += dot(source, grads_ref[i])
    grad = dot(grads_ref[0], gathered(wk), NT) + dot(grads_ref[1], gathered(wv), NT)
    grad = short(grad)

    @pl.when(pl.program_id(0) == place[2])
    def _():
        own_ref[...] = grad

    @pl.when(pl.program_id(0) != place[2])
    def _():
        away_ref[...] = grad

    @at_end
    def _():
        for i in range(2):
            deal(place, False, keep_ref, send_ref, shard_pieces(weight_ref.at[i], i))


def source_back(place, grads, source, weights, width):
    rows = grads.shape[1]
    return call(
        source_back_kernel,
        (rows // width,),
        [
            pl.BlockSpec((2, width, MODEL), lambda i, *_: (0, i, 0)),
            by_rows(width),
            weight_at(5),
            weight_at(6),
        ],
        kept_or_sent(width) + [slots_at(2)] * 2,
        [struct((width, MODEL), jnp.bfloat16)] * 2 + [buffer_of(2)] * 2,
        scratch=[pltpu.VMEM((2, MODEL, MODEL), jnp.float32)],
        prefetch=1,
    )(place, grads, source, weights, weights)


def pairs(bit):
    return [(i, i ^ bit) for i in range(16)]


def swap(values):
    return lax.ppermute(values, "ctx", [(0, 1), (1, 0)])


def over_x(values):
    return lax.ppermute(values, "fsdp", pairs(2))


def over_core(values):
    return lax.ppermute(values, "fsdp", pairs(1))


def tie(*values):
    return lax.optimization_barrier(values)


def lot_specs(lot, first, second, spread, z_of, depth=1):
    specs = []
    for keep, _ in lot:
        slots, rows = keep.shape[3:5]
        block = (1, spread, depth, slots, rows, MODEL)
        specs += [
            pl.BlockSpec(block, lambda i, place: (first, second, z_of(i, place), 0, 0, 0))
        ] * 2
    return specs


def slots_of(lot):
    return sum(keep.shape[3] for keep, _ in lot)


def in_order(i, place):
    return i


def from_own(i, place):
    return lax.rem(place[3] + i, 4)


def pair_sums(refs, count):
    return [wide(refs[2 * i][...]) + wide(refs[2 * i + 1][...]) for i in range(count)]


def depth_of(lots):
    return 4 if sum(slots_of(lot) for lot in lots) < 4 else 1


def ranges(sizes):
    starts = [sum(sizes[:i]) for i in range(len(sizes))]
    return [(start, start + size) for start, size in zip(starts, sizes)]


def overlaps(sources, pieces):
    for i, (s0, s1) in enumerate(ranges(sources)):
        for j, (p0, p1) in enumerate(ranges(pieces)):
            low, high = (max(s0, p0), min(s1, p1))
            if low < high:
                yield i, j, slice(low - s0, high - s0), slice(low - p0, high - p0)


def sizes_of(lot):
    return [keep.shape[3] for keep, _ in lot]


def first_sums(place, lots, cuts=None):
    cuts = cuts or [[slots_of(lot)] for lot in lots]

    def kernel(place_ref, *refs):
        refs = list(refs)
        outs = refs[-sum(len(cut) for cut in cuts) :]
        for lot, cut in zip(lots, cuts):
            values = pair_sums([refs.pop(0) for _ in range(2 * len(lot))], len(lot))
            pieces, outs = (outs[: len(cut)], outs[len(cut) :])
            for i, j, taken, put in overlaps(sizes_of(lot), cut):
                pieces[j][:, :, put] = short(values[i][0, :, :, taken])

    depth = depth_of(lots)
    shapes = [(2, 4, size, 32, MODEL) for cut in cuts for size in cut]
    outs = call(
        kernel,
        (4 // depth,),
        [spec for lot in lots for spec in lot_specs(lot, 1, 0, 2, in_order, depth)],
        [
            pl.BlockSpec((2, depth) + shape[2:], lambda i, place: (0, i, 0, 0, 0))
            for shape in shapes
        ],
        [struct(shape, jnp.bfloat16) for shape in shapes],
        prefetch=1,
    )(place, *[array for lot in lots for pair in lot for array in pair])
    return [outs[start:end] for start, end in ranges([len(cut) for cut in cuts])]


def second_sums(place, lots, firsts, cuts=None):
    cuts = cuts or [[slots_of(lot)] for lot in lots]

    def kernel(place_ref, *refs):
        refs = list(refs)
        outs = refs[-sum(len(cut) for cut in cuts) :]
        for lot, first, cut in zip(lots, firsts, cuts):
            values = pair_sums([refs.pop(0) for _ in range(2 * len(lot))], len(lot))
            received = [wide(refs.pop(0)[0]) for _ in first]
            received = received[0] if len(first) == 1 else jnp.concatenate(received, axis=1)
            pieces, outs = (outs[: len(cut)], outs[len(cut) :])
            spots = ranges(sizes_of(lot))
            for i, j, taken, put in overlaps(sizes_of(lot), cut):
                there = received[:, spots[i][0] + taken.start : spots[i][0] + taken.stop]
                pieces[j][:, put] = short(values[i][0, 0, :, taken] + there)

    depth = depth_of(lots)
    specs, arrays = ([], [])
    for lot, first in zip(lots, firsts):
        specs += lot_specs(lot, 0, 1, 1, in_order, depth)
        specs += [
            pl.BlockSpec((1, depth) + piece.shape[2:], lambda i, place: (1, i, 0, 0, 0))
            for piece in first
        ]
        arrays += [array for pair in lot for array in pair] + list(first)
    shapes = [(4, size, 32, MODEL) for cut in cuts for size in cut]
    outs = call(
        kernel,
        (4 // depth,),
        specs,
        [pl.BlockSpec((depth,) + shape[1:], lambda i, place: (i, 0, 0, 0)) for shape in shapes],
        [struct(shape, jnp.bfloat16) for shape in shapes],
        prefetch=1,
    )(place, *arrays)
    return [outs[start:end] for start, end in ranges([len(cut) for cut in cuts])]


def third_sums(place, lots, firsts, seconds):
    def kernel(place_ref, *refs):
        refs = list(refs)
        out = refs[-1]
        start = 0
        for lot, first, second in zip(lots, firsts, seconds):
            values = pair_sums([refs.pop(0) for _ in range(2 * len(lot))], len(lot))
            parts_of = (
                [wide(refs.pop(0)[0, 0]) for _ in first],
                [wide(refs.pop(0)[0]) for _ in second],
            )
            received = sum(p[0] if len(p) == 1 else jnp.concatenate(p, axis=0) for p in parts_of)
            for value, (s0, s1) in zip(values, ranges(sizes_of(lot))):
                out[0, start + s0 : start + s1] = short(value[0, 0, 0] + received[s0:s1])
            start += slots_of(lot)

    specs, arrays = ([], [])
    for lot, first, second in zip(lots, firsts, seconds):
        specs += lot_specs(lot, 0, 0, 1, in_order)
        specs += [
            pl.BlockSpec((1, 1) + piece.shape[2:], lambda i, place: (0, i, 0, 0, 0))
            for piece in first
        ]
        specs += [
            pl.BlockSpec((1,) + piece.shape[1:], lambda i, place: (i, 0, 0, 0))
            for piece in second
        ]
        arrays += [array for pair in lot for array in pair] + list(first) + list(second)
    shape = (4, sum(slots_of(lot) for lot in lots), 32, MODEL)
    return call(
        kernel,
        (4,),
        specs,
        [pl.BlockSpec((1,) + shape[1:], lambda i, place: (i, 0, 0, 0))],
        [struct(shape, jnp.bfloat16)],
        prefetch=1,
    )(place, *arrays)[0]


def direct_sums(place, lot, first):
    (keep, core) = lot
    slots = keep.shape[3]

    def kernel(place_ref, keep_ref, core_ref, *refs):
        received = [wide(ref[...]) for ref in refs[:-1]]
        received = received[0] if len(first) == 1 else jnp.concatenate(received, axis=2)
        total = wide(keep_ref[0]) + wide(core_ref[0]) + received
        refs[-1][0] = short(total[:, 0])

    block = (1, 2, 1, slots, 32, MODEL)
    shape = (4, 2, slots, 32, MODEL)
    return call(
        kernel,
        (4,),
        [pl.BlockSpec(block, lambda i, place: (0, 0, i, 0, 0, 0))] * 2
        + [
            pl.BlockSpec((2, 1) + piece.shape[2:], lambda i, place: (0, i, 0, 0, 0))
            for piece in first
        ],
        [pl.BlockSpec((1,) + shape[1:], lambda i, place: (i, 0, 0, 0, 0))],
        [struct(shape, jnp.bfloat16)],
        prefetch=1,
    )(place, keep, core, *first)[0]


def over_z(values):
    groups = [[first + 4 * z for z in range(4)] for first in range(4)]
    return lax.psum_scatter(values, "fsdp", scatter_dimension=0, axis_index_groups=groups)


def both_parts(total, other):
    low = lax.axis_index("ctx") == 0
    return wide(jnp.stack([jnp.where(low, total, other), jnp.where(low, other, total)], axis=1))


def columns(shares, start, stop):
    part = shares[start:stop].reshape(stop - start, -1, MODEL)
    return jnp.concatenate(list(part), axis=1)


def feed_shares(lots):
    inner = [lot[:2].reshape(2, 64, 8, 128).transpose(1, 0, 2, 3).reshape(64, 16, 128) for lot in lots]
    inner = jnp.stack(inner, axis=2).reshape(64, 4 * MODEL)
    outer = [lot[2:].transpose(1, 0, 2, 3).reshape(128, MODEL) for lot in lots]
    return inner, jnp.concatenate(outer)


def whole_packs(mesh):
    return mesh.shape["ctx"] == 2 and mesh.shape["fsdp"] == 16


def whole_pack_body(
    tokens,
    encoded,
    cotangent,
    order,
    target_lengths,
    source_lengths,
    self_project,
    self_output,
    cross_query,
    cross_source,
    cross_output,
    feed_in,
    feed_out,
    norm_gain,
    norm_bias,
):
    rows = tokens.shape[2]
    pack_rows, source_rows = (2 * rows, 2 * encoded.shape[2])
    first_rows = 3 * pack_rows // 4
    width = rows // 2
    mine = lax.axis_index("ctx")
    spot = lax.axis_index("fsdp")
    z = spot // 4
    place = jnp.stack([spot % 2, spot // 2 % 2, mine, z]).astype(jnp.int32)
    part = self_project.shape[0]

    norms = jnp.pad(jnp.concatenate([norm_gain, norm_bias]), ((0, 10), (0, MODEL - part)))
    attention_shard, feed_shard = pack(
        (self_project, self_output, cross_query, cross_source, cross_output, feed_in, feed_out),
        norms,
    )
    weights = lax.all_gather(attention_shard, "fsdp", axis=0)
    norms = wide(weights[:, 8 * part : 8 * part + 8, :part])
    norms = norms.transpose(1, 0, 2).reshape(8, MODEL)

    def both_halves(array):
        own = lax.dynamic_index_in_dim(array, mine, 0, False)[0]
        return own, swap(lax.dynamic_index_in_dim(array, 1 - mine, 0, False)[0])

    places = lax.dynamic_index_in_dim(order, mine, 0, False)[0]
    holds = places[::width] // width
    found = jnp.argsort(holds).astype(jnp.int32)
    held = jnp.where(found // 2 == mine, found % 2, 2 + found % 2)

    def from_both(own, other):
        low = mine == 0
        return jnp.stack([jnp.where(low, own, other), jnp.where(low, other, own)])[:, None]

    halves = jnp.concatenate(both_halves(tokens))
    own, other = both_halves(encoded)
    source = jnp.concatenate([jnp.where(mine == 0, own, other), jnp.where(mine == 0, other, own)])
    lengths = lax.dynamic_index_in_dim(target_lengths, mine, 0, False)[0]
    target_docs = docs_of(jnp.arange(pack_rows, dtype=jnp.int32), lengths)
    lengths = lax.dynamic_index_in_dim(source_lengths, mine, 0, False)[0]
    source_docs = docs_of(jnp.arange(source_rows, dtype=jnp.int32), lengths)
    docs = lengths.shape[0]
    marks = query_marks(target_docs)
    target_marks = key_marks(target_docs, docs)
    source_marks = key_marks(source_docs, docs)
    cotangent_own, cotangent_away = (
        lax.dynamic_index_in_dim(cotangent, which, 0, False)[0] for which in (mine, 1 - mine)
    )
    tied = (feed_shard, halves, source, marks, target_marks, source_marks)
    feed_shard, halves, source, marks, target_marks, source_marks, *cotangents = tie(
        *tied, cotangent_own, cotangent_away
    )
    feed_weights = lax.all_gather(feed_shard, "fsdp", axis=0)

    reach = source_rows // 2

    first, query, keys, values = enter(held, halves, norms, weights, width)
    query, cotangents[1] = tie(query, cotangents[1])
    cotangents[1] = swap(cotangents[1])
    plan = self_plan(first_rows, pack_rows, width)
    self_mixed, self_extra = attend(plan, query, keys, values, marks, target_marks)
    self_mixed, source = tie(self_mixed, source)
    cross_keys, cross_values = source_pairs(source, weights, source_rows // 2)
    after_self, second, cross_queries = between(held, self_mixed, halves, norms, weights, width)
    plan = cross_plan(first_rows, pack_rows, reach, source_rows, width)
    cross_mixed, cross_extra = attend(
        plan, cross_queries, cross_keys, cross_values, marks, source_marks
    )
    after_cross, third, grad_out = before_feed(
        held, cross_mixed, after_self, *cotangents, norms, weights, width
    )

    out, back, lot_a, lot_b = feed(place, third, grad_out, feed_weights)
    lot_a, lot_b = ([(lot[0], over_core(lot[1]))] for lot in (lot_a, lot_b))
    result, result_away, grad_after_cross, grad_cross_mixed, sums_two, *part_out = after_feed(
        held, place, after_cross, out, back, grad_out, cross_mixed, norms, weights, width
    )
    (first_a,), (first_b,) = first_sums(place, [lot_a, lot_b])
    first_ab = (first_a, first_b)
    grad_cross_mixed, part_out[1], *first_ab = tie(grad_cross_mixed, part_out[1], *first_ab)
    first_ab = (over_x(first_ab[0]), swap(first_ab[1]))
    part_out[1] = over_core(part_out[1])
    plan = cross_plan(first_rows, pack_rows, reach, source_rows, width)
    grad_cross_queries, grad_source = attend_back(
        plan,
        cross_queries,
        cross_keys,
        cross_values,
        cross_extra,
        source_marks,
        cross_mixed,
        grad_cross_mixed,
        False,
    )
    grad_source, part_out[1], *first_ab = tie(grad_source, part_out[1], *first_ab)
    encoded_own, encoded_away, *part_source = source_back(
        place, grad_source, source, weights, source_rows // 2
    )
    first_ab = [[first] for first in first_ab]
    second_ab = [second for (second,) in second_sums(place, [lot_a, lot_b], first_ab)]
    grad_cross_queries, encoded_away, *second_ab = tie(
        grad_cross_queries, encoded_away, *second_ab
    )
    second_ab = (swap(second_ab[0]), over_x(second_ab[1]))
    grad_after_self, grad_self_mixed, sums_one, *part_middle = middle(
        place,
        grad_cross_queries,
        second,
        after_self,
        grad_after_cross,
        self_mixed,
        norms,
        weights,
        width,
    )
    grad_self_mixed, part_source[1], part_middle[1], *second_ab = tie(
        grad_self_mixed, part_source[1], part_middle[1], *second_ab
    )
    part_source[1], part_middle[1] = (over_core(part_source[1]), over_core(part_middle[1]))
    third_ab = third_sums(place, [lot_a, lot_b], first_ab, [[second] for second in second_ab])
    lot_c = [part_out, part_source, part_middle]
    ((first_c,),) = first_sums(place, [lot_c])
    grad_self_mixed, first_c, result_away, encoded_away, third_ab = tie(
        grad_self_mixed, first_c, result_away, encoded_away, third_ab
    )
    first_c = over_x(first_c)
    result_away, encoded_away = (swap(result_away), swap(encoded_away))
    total_ab = over_z(third_ab)
    plan = self_plan(first_rows, pack_rows, width)
    grads = attend_back(
        plan,
        query,
        keys,
        values,
        self_extra,
        target_marks,
        self_mixed,
        grad_self_mixed,
        True,
    )
    grads, first_c, result_away, encoded_away, total_ab = tie(
        grads, first_c, result_away, encoded_away, total_ab
    )
    (second_c,) = second_sums(place, [lot_c], [[first_c]], [[3, 2]])
    grads, total_ab, *second_c = tie(grads, total_ab, *second_c)
    second_c[0] = swap(second_c[0])
    lot_d = list(project_grad(place, first, grads))
    lot_d[1], total_ab, *second_c = tie(lot_d[1], total_ab, *second_c)
    second_c[1] = swap(second_c[1])
    lot_d = [(lot_d[0], over_core(lot_d[1]))]
    (first_d,) = first_sums(place, [lot_d], [[2, 1]])
    second_c[1], *first_d = tie(second_c[1], *first_d)
    third_c = third_sums(place, [lot_c], [[first_c]], [second_c])
    grads, third_c, total_ab, *first_d = tie(grads, third_c, total_ab, *first_d)
    total_c, other_ab = (over_z(third_c), swap(total_ab))
    first_d[0] = over_x(first_d[0])
    tokens_own, tokens_away, sums_zero = finish(
        held, grads, halves, grad_after_self, norms, weights, width
    )
    tokens_own, sums_zero, other_ab, *first_d = tie(tokens_own, sums_zero, other_ab, *first_d)
    first_d[1] = over_x(first_d[1])
    tokens_other = swap(tokens_away)
    third_d = direct_sums(place, lot_d[0], first_d)
    sums_zero, other_ab, third_d, result, result_away, encoded_own, encoded_away = tie(
        sums_zero, other_ab, third_d, result, result_away, encoded_own, encoded_away
    )
    total_d = over_z(third_d)
    result = from_both(result, result_away)
    grad_encoded = from_both(encoded_own, encoded_away)
    sums = jnp.concatenate([sums_zero[:2], sums_one[:2], sums_two[:2]])
    for bit in (1, 2, 4, 8):
        sums = sums + lax.ppermute(sums, "fsdp", pairs(bit))
    sums = sums + swap(sums)
    share_ab = both_parts(total_ab, other_ab)
    feed_in_grad, feed_out_grad = feed_shares((share_ab[:4], share_ab[4:]))
    share_c = both_parts(total_c, swap(total_c))
    grad_tokens = from_both(tokens_own, tokens_other)
    tied = (sums, result, grad_encoded, grad_tokens, feed_in_grad, feed_out_grad, share_c, total_d)
    sums, result, grad_encoded, grad_tokens, feed_in_grad, feed_out_grad, share_c, total_d = tie(
        *tied
    )
    share_d = (wide(total_d) + wide(swap(total_d))).transpose(1, 0, 2, 3)

    sums = lax.dynamic_slice_in_dim(sums, spot * part, part, 1)

    return (
        result,
        grad_tokens,
        grad_encoded,
        columns(share_d, 0, 3),
        columns(share_c, 4, 5),
        columns(share_c, 3, 4),
        columns(share_c, 1, 3),
        columns(share_c, 0, 1),
        feed_in_grad,
        feed_out_grad,
        sums[0::2],
        sums[1:4:2],
        sums[5],
    )


def solution(mesh):
    chosen = whole_pack_body if whole_packs(mesh) else body
    return jax.shard_map(
        chosen,
        mesh=mesh,
        in_specs=(
            P(None, "fsdp", "ctx", None),
            P(None, "fsdp", "ctx", None),
            P(None, "fsdp", "ctx", None),
            P(None, "fsdp", None),
            P(None, "fsdp", None),
            P(None, "fsdp", None),
            P("fsdp", None),
            P("fsdp", None),
            P("fsdp", None),
            P("fsdp", None),
            P("fsdp", None),
            P("fsdp", None),
            P("fsdp", None),
            P(None, "fsdp"),
            P(None, "fsdp"),
        ),
        out_specs=(
            P(None, "fsdp", "ctx", None),
            P(None, "fsdp", "ctx", None),
            P(None, "fsdp", "ctx", None),
            P("fsdp", None),
            P("fsdp", None),
            P("fsdp", None),
            P("fsdp", None),
            P("fsdp", None),
            P("fsdp", None),
            P("fsdp", None),
            P(None, "fsdp"),
            P(None, "fsdp"),
            P("fsdp"),
        ),
        check_vma=False,
    )
```

profile of v0, /device:TPU:0, one launch (start us, length us, event | category | flops | bytes accessed | tf_op | source)
XLA Modules:
  0.0 685.5 jit_solution(16124314948475824025)
XLA Ops:
  7.3 1.5 fusion.8.refs_7_
  8.7 3.1 shard_map.246
  13.0 3.0 collective-permute-start.1
  16.0 3.4 dynamic-slice_bitcast_fusion.3
  20.5 4.5 dynamic-slice_bitcast_fusion
  27.4 12.9 %collective-permute-done.1 = bf16[512,1024]{1,0:T(8,128)(2,1)} collective-permute-done((bf16[512,1024]{1,0:T(8,128)(2,1)}, bf16[512,1024]{1,0:T(8,128)(2,1)}, u32[]{:S(2)}, u32[]{:S(2)}) %collective-permute-start.1) | collective-permute-done | bytes 1048608 | tf_op jit(solution)/shard_map/ppermute | solution.py:1219
  40.3 1.7 bitcast_select_fusion.1
  41.9 1.5 pad_maximum_fusion.1.source_ref
  43.4 29.6 %collective-permute-done = bf16[768,1024]{1,0:T(8,128)(2,1)S(1)} collective-permute-done((bf16[768,1024]{1,0:T(8,128)(2,1)}, bf16[768,1024]{1,0:T(8,128)(2,1)S(1)}, u32[]{:S(2)}, u32[]{:S(2)}) %collective-permute-start) | collective-permute-done | bytes 1572896 | tf_op jit(solution)/shard_map/ppermute | solution.py:1219
  73.0 2.0 pad_maximum_fusion.tokens_ref
  77.0 29.3 %all-gather.5.cloned.1.call-done = bf16[8448,1024]{1,0:T(8,128)(2,1)} async-done(((bf16[528,1024]{1,0:T(8,128)(2,1)}), bf16[8448,1024]{1,0:T(8,128)(2,1)}) %all-gather.5.cloned.1.call-update) | async-done | bytes 17301520 | tf_op jit(solution)/shard_map/all_gather | solution.py:1470
  107.8 17.0 %shard_map.247 = (bf16[1536,1024]{1,0:T(8,128)(2,1)}, bf16[1536,1024]{1,0:T(8,128)(2,1)}, bf16[1536,1024]{1,0:T(8,128)(2,1)}, bf16[1536,1024]{1,0:T(8,128)(2,1)}) custom-call(s32[4]{0:T(128)} %compare_select_fusion.3.held, bf16[1536,1024]{1,0:T(8,128)(2,1)} %pad_maximum_fusion.tokens_ref, f32[8,1024]{1,0:T(8,128)} %reshape.150.norm_ref, ...), custom_call_target="tpu_custom_call" | custom-call | flops 1024 | bytes 1024 | tf_op jit(solution)/shard_map/pallas_call | solution.py:799
  124.7 1.5 collective-permute-start.2
  126.8 27.9 %shard_map.248 = (bf16[1536,1024]{1,0:T(8,128)(2,1)}, bf16[1536,1024]{1,0:T(8,128)(2,1)}) custom-call(bf16[1536,1024]{1,0:T(8,128)(2,1)} %get-tuple-element.150.q_ref, bf16[1536,1024]{1,0:T(8,128)(2,1)} %get-tuple-element.151.k_ref, bf16[1536,1024]{1,0:T(8,128)(2,1)} %get-tuple-element.152.v_ref, bf16[1536,128]{1,0:T(8,128)(2,1)} %fusion.qd_ref, ...), custom_call_target="tpu_custom_call" | custom-call | flops 1024 | bytes 1024 | tf_op jit(solution)/shard_map/pallas_call | solution.py:591
  154.7 8.4 %shard_map.250 = (bf16[1024,1024]{1,0:T(8,128)(2,1)}, bf16[1024,1024]{1,0:T(8,128)(2,1)}) custom-call(bf16[1024,1024]{1,0:T(8,128)(2,1)} %pad_maximum_fusion.1.source_ref, bf16[16,528,1024]{2,1,0:T(8,128)(2,1)} %bitcast.111, bf16[16,528,1024]{2,1,0:T(8,128)(2,1)} %bitcast.112), custom_call_target="tpu_custom_call" | custom-call | flops 1024 | bytes 1024 | tf_op jit(solution)/shard_map/pallas_call | solution.py:816
  163.1 13.4 %shard_map.249 = (f32[1536,1024]{1,0:T(8,128)}, bf16[1536,1024]{1,0:T(8,128)(2,1)}, bf16[1536,1024]{1,0:T(8,128)(2,1)}) custom-call(s32[4]{0:T(128)} %compare_select_fusion.3.held, bf16[1536,1024]{1,0:T(8,128)(2,1)} %get-tuple-element.158.mixed_ref.self_ref.out_ref, bf16[1536,1024]{1,0:T(8,128)(2,1)} %pad_maximum_fusion.tokens_ref, ...), custom_call_target="tpu_custom_call" | custom-call | flops 1024 | bytes 1024 | tf_op jit(solution)/shard_map/pallas_call | solution.py:834
  176.5 27.5 %shard_map.251 = (bf16[1536,1024]{1,0:T(8,128)(2,1)}, bf16[1536,1024]{1,0:T(8,128)(2,1)}) custom-call(bf16[1536,1024]{1,0:T(8,128)(2,1)} %get-tuple-element.159.q_ref, bf16[1024,1024]{1,0:T(8,128)(2,1)} %get-tuple-element.161.k_ref, bf16[1024,1024]{1,0:T(8,128)(2,1)} %get-tuple-element.162.v_ref, bf16[1536,128]{1,0:T(8,128)(2,1)} %fusion.qd_ref, ...), custom_call_target="tpu_custom_call" | custom-call | flops 1024 | bytes 1024 | tf_op jit(solution)/shard_map/pallas_call | solution.py:591
  204.1 1.2 copy-done.12
  205.2 13.2 %shard_map.252 = (f32[1536,1024]{1,0:T(8,128)}, bf16[1536,1024]{1,0:T(8,128)(2,1)}, bf16[1536,1024]{1,0:T(8,128)(2,1)}) custom-call(s32[4]{0:T(128)} %compare_select_fusion.3.held, bf16[1536,1024]{1,0:T(8,128)(2,1)} %get-tuple-element.165.mixed_ref.cross_ref.out_ref, f32[1536,1024]{1,0:T(8,128)} %get-tuple-element.166.base_ref.after_ref, ...), custom_call_target="tpu_custom_call" | custom-call | flops 1024 | bytes 1024 | tf_op jit(solution)/shard_map/pallas_call | solution.py:862
  218.4 113.4 %shard_map.253 = (f32[1536,1024]{1,0:T(8,128)}, f32[1536,1024]{1,0:T(8,128)}, bf16[2,2,4,4,32,1024]{5,4,3,2,1,0:T(8,128)(2,1)}, bf16[2,2,4,4,32,1024]{5,4,3,2,1,...) custom-call(s32[4]{0:T(128)} %pad_add_fusion.place_ref.place, ...), custom_call_target="tpu_custom_call" | custom-call | flops 1024 | bytes 1024 | tf_op jit(solution)/shard_map/pallas_call | solution.py:983
  332.7 21.6 %shard_map.254 = (bf16[768,1024]{1,0:T(8,128)(2,1)}, bf16[768,1024]{1,0:T(8,128)(2,1)}, f32[1536,1024]{1,0:T(8,128)}, bf16[1536,1024]{1,0:T(8,128)(2,1)}, f32[8,...) custom-call(s32[4]{0:T(128)} %compare_select_fusion.3.held, ...), custom_call_target="tpu_custom_call" | custom-call | flops 1024 | bytes 1024 | tf_op jit(solution)/shard_map/pallas_call | solution.py:1063
  354.3 1.9 copy-done.2
  356.2 6.7 shard_map.255
  364.7 45.4 %shard_map.256 = (bf16[1536,1024]{1,0:T(8,128)(2,1)}, bf16[2,1024,1024]{2,1,0:T(8,128)(2,1)}) custom-call(bf16[1536,1024]{1,0:T(8,128)(2,1)} %get-tuple-element.159.q_ref, bf16[1024,1024]{1,0:T(8,128)(2,1)} %get-tuple-element.161.k_ref, bf16[1024,1024]{1,0:T(8,128)(2,1)} %get-tuple-element.162.v_ref, bf16[1536,1024]{1,0:T(8,128)(2,1)} %get-tuple-element.164.extra_ref, ...), custom_call_target="tpu_custom_call" | custom-call | flops 1024 | bytes 1024 | tf_op jit(solution)/shard_map/pallas_call | solution.py:613
  411.4 17.2 %shard_map.257 = (bf16[512,1024]{1,0:T(8,128)(2,1)}, bf16[512,1024]{1,0:T(8,128)(2,1)}, bf16[2,2,4,2,32,1024]{5,4,3,2,1,0:T(8,128)(2,1)}, bf16[2,2,4,2,32,1024]{5,4,3,2,1,0:T(8,128)(2,1)}) custom-call(s32[4]{0:T(128)} %pad_add_fusion.place_ref.place, bf16[2,1024,1024]{2,1,0:T(8,128)(2,1)} %get-tuple-element.189.grads_ref, ...), custom_call_target="tpu_custom_call" | custom-call | flops 1024 | bytes 1024 | tf_op jit(solution)/shard_map/pallas_call | solution.py:1198
  428.7 5.4 shard_map.258
  436.1 26.2 %shard_map.259 = (f32[1536,1024]{1,0:T(8,128)}, bf16[1536,1024]{1,0:T(8,128)(2,1)}, f32[8,1024]{1,0:T(8,128)}, bf16[2,2,4,2,32,1024]{5,4,3,2,1,0:T(8,128)(2,1)}, bf16[2,2,4,2,32,1024]{5,4,3,2,1,0:T(8,128)(2,1)}) custom-call(s32[4]{0:T(128)} %pad_add_fusion.place_ref.place, bf16[1536,1024]{1,0:T(8,128)(2,1)} %get-tuple-element.195.grad_ref, ...), custom_call_target="tpu_custom_call" | custom-call | flops 1024 | bytes 1024 | tf_op jit(solution)/shard_map/pallas_call | solution.py:1107
  463.6 6.1 shard_map.261
  469.9 1.2 copy-done.3
  471.1 5.4 shard_map.260
  476.5 1.2 collective-permute-start.12
  479.8 49.8 %shard_map.262.right_ref.grads_ref = bf16[3,1536,1024]{2,1,0:T(8,128)(2,1)} custom-call(bf16[1536,1024]{1,0:T(8,128)(2,1)} %get-tuple-element.150.q_ref, bf16[1536,1024]{1,0:T(8,128)(2,1)} %get-tuple-element.151.k_ref, bf16[1536,1024]{1,0:T(8,128)(2,1)} %get-tuple-element.152.v_ref, bf16[1536,1024]{1,0:T(8,128)(2,1)} %get-tuple-element.155.extra_ref, ...), custom_call_target="tpu_custom_call" | custom-call | flops 1024 | bytes 1024 | tf_op jit(solution)/shard_map/pallas_call | solution.py:613
  529.6 6.3 collective-permute-done.14
  536.9 1.5 copy-done.5
  538.4 4.8 shard_map.263
  544.0 17.8 %shard_map.264 = (bf16[2,2,4,3,32,1024]{5,4,3,2,1,0:T(8,128)(2,1)}, bf16[2,2,4,3,32,1024]{5,4,3,2,1,0:T(8,128)(2,1)}) custom-call(s32[4]{0:T(128)} %pad_add_fusion.place_ref.place, bf16[1536,1024]{1,0:T(8,128)(2,1)} %get-tuple-element.225.left_ref, bf16[3,1536,1024]{2,1,0:T(8,128)(2,1)} %shard_map.262.right_ref.grads_ref), custom_call_target="tpu_custom_call" | custom-call | flops 1024 | bytes 1024 | tf_op jit(solution)/shard_map/pallas_call | solution.py:1131
  561.9 1.2 collective-permute-start.16
  563.2 4.6 collective-permute-done.17.refs_1_.core_ref
  567.8 1.7 copy-done.4
  569.4 3.9 shard_map.265
  573.4 2.9 collective-permute-done.16.refs_8_
  577.1 5.3 shard_map.266
  582.5 1.5 collective-permute-start.19
  584.7 20.9 %shard_map.267 = (bf16[768,1024]{1,0:T(8,128)(2,1)}, bf16[768,1024]{1,0:T(8,128)(2,1)}, f32[8,1024]{1,0:T(8,128)}) custom-call(s32[4]{0:T(128)} %compare_select_fusion.3.held, bf16[3,1536,1024]{2,1,0:T(8,128)(2,1)} %shard_map.262.right_ref.grads_ref, bf16[1536,1024]{1,0:T(8,128)(2,1)} %pad_maximum_fusion.tokens_ref, ...), custom_call_target="tpu_custom_call" | custom-call | flops 1024 | bytes 1024 | tf_op jit(solution)/shard_map/pallas_call | solution.py:1156
  605.7 1.6 collective-permute-done.19.refs_0_
  607.2 1.4 collective-permute-start.20
  610.9 9.2 %collective-permute-done.20.refs_1_ = bf16[2,4,1,32,1024]{4,3,2,1,0:T(8,128)(2,1)S(1)} collective-permute-done((bf16[2,4,1,32,1024]{4,3,2,1,0:T(8,128)(2,1)}, bf16[2,4,1,32,1024]{4,3,2,1,0:T(8,128)(2,1)S(1)}, u32[]{:S(2)}, u32[]{:S(2)}) %collective-permute-start.20) | collective-permute-done | bytes 524320 | tf_op jit(solution)/shard_map/ppermute | solution.py:1223
  620.9 5.0 shard_map.268
  627.1 1.2 fusion.12
  630.1 1.3 copy-done.13
  631.3 1.7 select_bitcast_fusion.3
  633.1 12.3 %collective-permute-done.26 = bf16[768,1024]{1,0:T(8,128)(2,1)} collective-permute-done((bf16[768,1024]{1,0:T(8,128)(2,1)}, bf16[768,1024]{1,0:T(8,128)(2,1)}, u32[]{:S(2)}, u32[]{:S(2)}) %collective-permute-start.26) | collective-permute-done | bytes 1572896 | tf_op jit(solution)/shard_map/ppermute | solution.py:1219
  645.4 1.6 select_bitcast_fusion.1
  647.0 1.9 maximum_bitcast_fusion.1
  649.6 1.9 maximum_bitcast_fusion
  651.6 1.4 collective-permute-done.22
  652.9 1.7 collective-permute-start.23
  654.6 1.2 collective-permute-start.27
  655.8 1.5 maximum_bitcast_fusion.2
  657.3 1.6 collective-permute-done.23
  658.9 1.7 collective-permute-start.24
  661.6 2.1 collective-permute-done.24
  665.5 1.8 reshape.146
  672.2 5.4 collective-permute-done.28
  (163 shorter events, 37.2 us)
Async XLA Ops:
  7.2 68.4 %copy-start = (s32[2,1,1536]{2,1,0:T(1,128)S(1)}, s32[2,1,1536]{2,1,0:T(1,128)}, u32[]{:S(2)}) copy-start(s32[2,1,1536]{2,1,0:T(1,128)} %param.18) | copy-start | bytes 36868
  7.2 4.7 copy-start.9
  7.2 99.1 %all-gather.5.cloned.1.call-start = ((), (), s32[]{:S(2)}) async-start(), calls=%async_computation.6 | async-start | bytes 18382848 | tf_op jit(solution)/shard_map/all_gather | solution.py:1470
  11.9 206.6 %all-gather.7.cloned.1.call-start = ((), (), s32[]{:S(2)}) async-start(), calls=%async_computation.7 | async-start | bytes 18382848 | tf_op jit(solution)/shard_map/all_gather | solution.py:1505
  13.0 27.3 %collective-permute-start.1 = (bf16[512,1024]{1,0:T(8,128)(2,1)}, bf16[512,1024]{1,0:T(8,128)(2,1)}, u32[]{:S(2)}, u32[]{:S(2)}) collective-permute-start(bf16[512,1024]{1,0:T(8,128)(2,1)} %dynamic-slice_bitcast_fusion.4), channel_id=1, source_target_pairs={{0,16},{16,0},{1,17},{17,1},{2,18},{18,2},{3,19},{19,3},{4,20},{20... | collective-permute-start | bytes 3145736 | tf_op jit(solution)/shard_map/ppermute | solution.py:1219
  16.0 3.4 copy-start.28
  16.0 3.4 copy-start.29
  19.3 53.7 %collective-permute-start = (bf16[768,1024]{1,0:T(8,128)(2,1)}, bf16[768,1024]{1,0:T(8,128)(2,1)S(1)}, u32[]{:S(2)}, u32[]{:S(2)}) collective-permute-start(bf16[768,1024]{1,0:T(8,128)(2,1)} %get-tuple-element.349), channel_id=1, source_target_pairs={{0,16},{16,0},{1,17},{17,1},{2,18},{18,2},{3,19},{19,3},{4,20},{20... | collective-permute-start | bytes 4718600 | tf_op jit(solution)/shard_map/ppermute | solution.py:1219
  75.0 461.9 %reduce-scatter.4.cloned.1.call-start = ((), (), s32[]{:S(2)}) async-start(), calls=%async_computation.3 | async-start | bytes 2621440 | tf_op jit(solution)/shard_map/reduce_scatter | solution.py:1414
  107.8 17.0 %copy-start.15 = (bf16[768,1024]{1,0:T(8,128)(2,1)S(1)}, bf16[768,1024]{1,0:T(8,128)(2,1)}, u32[]{:S(2)}) copy-start(bf16[768,1024]{1,0:T(8,128)(2,1)} %get-tuple-element.168) | copy-start | bytes 4718596
  124.7 79.3 %collective-permute-start.2 = (bf16[768,1024]{1,0:T(8,128)(2,1)S(1)}, bf16[768,1024]{1,0:T(8,128)(2,1)S(1)}, u32[]{:S(2)}, u32[]{:S(2)}) collective-permute-start(bf16[768,1024]{1,0:T(8,128)(2,1)S(1)} %copy-done.15), channel_id=1, source_target_pairs={{0,16},{16,0},{1,17},{17,1},{2,18},{18,2},{3,19},{19,3},{4,20},{20... | collective-permute-start | bytes 4718600 | tf_op jit(solution)/shard_map/ppermute | solution.py:1219
  204.1 1.2 copy-start.12
  331.8 22.4 %collective-permute-start.3 = (bf16[2,2,4,4,32,1024]{5,4,3,2,1,0:T(8,128)(2,1)}, bf16[2,2,4,4,32,1024]{5,4,3,2,1,0:T(8,128)(2,1)S(1)}, u32[]{:S(2)}, u32[]{:S(2)}) collective-permute-start(bf16[2,2,4,4,32,1024]{5,4,3,2,1,0:T(8,128)(2,1)} %get-tuple-element.178), channel_id=1, source_target_pairs={{0,1},{1,0},{2,3},{3,2},{4,5},{5,4},{6,7},{7,6},{8,9},{9,8},{10,11... | collective-permute-start | bytes 12582920 | tf_op jit(solution)/shard_map/ppermute | solution.py:1227
  332.6 21.7 %collective-permute-start.4 = (bf16[2,2,4,4,32,1024]{5,4,3,2,1,0:T(8,128)(2,1)}, bf16[2,2,4,4,32,1024]{5,4,3,2,1,0:T(8,128)(2,1)}, u32[]{:S(2)}, u32[]{:S(2)}) collective-permute-start(bf16[2,2,4,4,32,1024]{5,4,3,2,1,0:T(8,128)(2,1)} %get-tuple-element.180), channel_id=1, source_target_pairs={{0,1},{1,0},{2,3},{3,2},{4,5},{5,4},{6,7},{7,6},{8,9},{9,8},{10,11... | collective-permute-start | bytes 12582920 | tf_op jit(solution)/shard_map/ppermute | solution.py:1227
  354.3 1.9 copy-start.2
  362.9 48.2 %collective-permute-start.6 = (bf16[2,4,4,32,1024]{4,3,2,1,0:T(8,128)(2,1)}, bf16[2,4,4,32,1024]{4,3,2,1,0:T(8,128)(2,1)S(1)}, u32[]{:S(2)}, u32[]{:S(2)}) collective-permute-start(bf16[2,4,4,32,1024]{4,3,2,1,0:T(8,128)(2,1)} %get-tuple-element.187), channel_id=1, source_target_pairs={{0,2},{1,3},{2,0},{3,1},{4,6},{5,7},{6,4},{7,5},{8,10},{9,11},{10,... | collective-permute-start | bytes 6291464 | tf_op jit(solution)/shard_map/ppermute | solution.py:1223
  363.9 47.5 %collective-permute-start.7 = (bf16[2,4,4,32,1024]{4,3,2,1,0:T(8,128)(2,1)}, bf16[2,4,4,32,1024]{4,3,2,1,0:T(8,128)(2,1)S(1)}, u32[]{:S(2)}, u32[]{:S(2)}) collective-permute-start(bf16[2,4,4,32,1024]{4,3,2,1,0:T(8,128)(2,1)} %get-tuple-element.188), channel_id=1, source_target_pairs={{0,16},{16,0},{1,17},{17,1},{2,18},{18,2},{3,19},{19,3},{4,20},{20... | collective-permute-start | bytes 6291464 | tf_op jit(solution)/shard_map/ppermute | solution.py:1219
  364.7 45.4 %collective-permute-start.5 = (bf16[2,2,4,1,32,1024]{5,4,3,2,1,0:T(8,128)(2,1)}, bf16[2,2,4,1,32,1024]{5,4,3,2,1,0:T(8,128)(2,1)S(1)}, u32[]{:S(2)}, u32[]{:S(2)}) collective-permute-start(bf16[2,2,4,1,32,1024]{5,4,3,2,1,0:T(8,128)(2,1)} %get-tuple-element.186), channel_id=1, source_target_pairs={{0,1},{1,0},{2,3},{3,2},{4,5},{5,4},{6,7},{7,6},{8,9},{9,8},{10,11... | collective-permute-start | bytes 3145736 | tf_op jit(solution)/shard_map/ppermute | solution.py:1227
  410.0 18.6 %copy-start.6 = (bf16[2,2,4,1,32,1024]{5,4,3,2,1,0:T(8,128)(2,1)}, bf16[2,2,4,1,32,1024]{5,4,3,2,1,0:T(8,128)(2,1)S(1)}, u32[]{:S(2)}) copy-start(bf16[2,2,4,1,32,1024]{5,4,3,2,1,0:T(8,128)(2,1)S(1)} %collective-permute-done.5.refs_1_) | copy-start | bytes 3145732
  411.1 17.6 %copy-start.7 = (bf16[2,4,4,32,1024]{4,3,2,1,0:T(8,128)(2,1)}, bf16[2,4,4,32,1024]{4,3,2,1,0:T(8,128)(2,1)S(1)}, u32[]{:S(2)}) copy-start(bf16[2,4,4,32,1024]{4,3,2,1,0:T(8,128)(2,1)S(1)} %collective-permute-done.6.refs_2_) | copy-start | bytes 6291460
  411.4 17.2 %copy-start.8 = (bf16[2,4,4,32,1024]{4,3,2,1,0:T(8,128)(2,1)}, bf16[2,4,4,32,1024]{4,3,2,1,0:T(8,128)(2,1)S(1)}, u32[]{:S(2)}) copy-start(bf16[2,4,4,32,1024]{4,3,2,1,0:T(8,128)(2,1)S(1)} %collective-permute-done.7.refs_5_.refs_6_) | copy-start | bytes 6291460
  434.1 28.2 %collective-permute-start.8 = (bf16[4,4,32,1024]{3,2,1,0:T(8,128)(2,1)}, bf16[4,4,32,1024]{3,2,1,0:T(8,128)(2,1)S(1)}, u32[]{:S(2)}, u32[]{:S(2)}) collective-permute-start(bf16[4,4,32,1024]{3,2,1,0:T(8,128)(2,1)} %get-tuple-element.201), channel_id=1, source_target_pairs={{0,16},{16,0},{1,17},{17,1},{2,18},{18,2},{3,19},{19,3},{4,20},{20... | collective-permute-start | bytes 3145736 | tf_op jit(solution)/shard_map/ppermute | solution.py:1219
  435.2 27.1 %collective-permute-start.9 = (bf16[4,4,32,1024]{3,2,1,0:T(8,128)(2,1)}, bf16[4,4,32,1024]{3,2,1,0:T(8,128)(2,1)S(1)}, u32[]{:S(2)}, u32[]{:S(2)}) collective-permute-start(bf16[4,4,32,1024]{3,2,1,0:T(8,128)(2,1)} %get-tuple-element.202), channel_id=1, source_target_pairs={{0,2},{1,3},{2,0},{3,1},{4,6},{5,7},{6,4},{7,5},{8,10},{9,11},{10,... | collective-permute-start | bytes 3145736 | tf_op jit(solution)/shard_map/ppermute | solution.py:1223
  462.3 1.0 copy-start.20
  462.3 1.3 copy-start.21
  462.3 7.4 %collective-permute-start.10 = (bf16[2,2,4,2,32,1024]{5,4,3,2,1,0:T(8,128)(2,1)}, bf16[2,2,4,2,32,1024]{5,4,3,2,1,0:T(8,128)(2,1)S(1)}, u32[]{:S(2)}, u32[]{:S(2)}) collective-permute-start(bf16[2,2,4,2,32,1024]{5,4,3,2,1,0:T(8,128)(2,1)} %get-tuple-element.207), channel_id=1, source_target_pairs={{0,1},{1,0},{2,3},{3,2},{4,5},{5,4},{6,7},{7,6},{8,9},{9,8},{10,11... | collective-permute-start | bytes 6291464 | tf_op jit(solution)/shard_map/ppermute | solution.py:1227
  462.4 7.5 %collective-permute-start.11 = (bf16[2,2,4,2,32,1024]{5,4,3,2,1,0:T(8,128)(2,1)}, bf16[2,2,4,2,32,1024]{5,4,3,2,1,0:T(8,128)(2,1)}, u32[]{:S(2)}, u32[]{:S(2)}) collective-permute-start(bf16[2,2,4,2,32,1024]{5,4,3,2,1,0:T(8,128)(2,1)} %get-tuple-element.209), channel_id=1, source_target_pairs={{0,1},{1,0},{2,3},{3,2},{4,5},{5,4},{6,7},{7,6},{8,9},{9,8},{10,11... | collective-permute-start | bytes 6291464 | tf_op jit(solution)/shard_map/ppermute | solution.py:1227
  469.7 1.3 copy-start.3
  476.5 178.1 %reduce-scatter.6.cloned.1.call-start = ((), (), s32[]{:S(2)}) async-start(), calls=%async_computation.4 | async-start | bytes 1638400 | tf_op jit(solution)/shard_map/reduce_scatter | solution.py:1414
  476.5 60.3 %collective-permute-start.12 = (bf16[2,4,5,32,1024]{4,3,2,1,0:T(8,128)(2,1)}, bf16[2,4,5,32,1024]{4,3,2,1,0:T(8,128)(2,1)S(1)}, u32[]{:S(2)}, u32[]{:S(2)}) collective-permute-start(bf16[2,4,5,32,1024]{4,3,2,1,0:T(8,128)(2,1)} %shard_map.260), channel_id=1, source_target_pairs={{0,2},{1,3},{2,0},{3,1},{4,6},{5,7},{6,4},{7,5},{8,10},{9,11},{10,... | collective-permute-start | bytes 7864328 | tf_op jit(solution)/shard_map/ppermute | solution.py:1223
  477.8 59.1 %collective-permute-start.13 = (bf16[768,1024]{1,0:T(8,128)(2,1)}, bf16[768,1024]{1,0:T(8,128)(2,1)}, u32[]{:S(2)}, u32[]{:S(2)}) collective-permute-start(bf16[768,1024]{1,0:T(8,128)(2,1)} %get-tuple-element.216), channel_id=1, source_target_pairs={{0,16},{16,0},{1,17},{17,1},{2,18},{18,2},{3,19},{19,3},{4,20},{20... | collective-permute-start | bytes 4718600 | tf_op jit(solution)/shard_map/ppermute | solution.py:1219
  478.7 57.2 %collective-permute-start.14 = (bf16[512,1024]{1,0:T(8,128)(2,1)}, bf16[512,1024]{1,0:T(8,128)(2,1)S(1)}, u32[]{:S(2)}, u32[]{:S(2)}) collective-permute-start(bf16[512,1024]{1,0:T(8,128)(2,1)} %get-tuple-element.217), channel_id=1, source_target_pairs={{0,16},{16,0},{1,17},{17,1},{2,18},{18,2},{3,19},{19,3},{4,20},{20... | collective-permute-start | bytes 3145736 | tf_op jit(solution)/shard_map/ppermute | solution.py:1219
  535.9 1.0 copy-start.17
  536.9 1.5 copy-start.5
  543.1 18.7 %collective-permute-start.15 = (bf16[4,3,32,1024]{3,2,1,0:T(8,128)(2,1)}, bf16[4,3,32,1024]{3,2,1,0:T(8,128)(2,1)S(1)}, u32[]{:S(2)}, u32[]{:S(2)}) collective-permute-start(bf16[4,3,32,1024]{3,2,1,0:T(8,128)(2,1)} %get-tuple-element.228), channel_id=1, source_target_pairs={{0,16},{16,0},{1,17},{17,1},{2,18},{18,2},{3,19},{19,3},{4,20},{20... | collective-permute-start | bytes 2359304 | tf_op jit(solution)/shard_map/ppermute | solution.py:1219
  544.0 17.9 %copy-start.31 = (bf16[4,2,32,1024]{3,2,1,0:T(8,128)(2,1)S(1)}, bf16[4,2,32,1024]{3,2,1,0:T(8,128)(2,1)}, u32[]{:S(2)}) copy-start(bf16[4,2,32,1024]{3,2,1,0:T(8,128)(2,1)} %get-tuple-element.231) | copy-start | bytes 1572868
  561.8 14.4 %copy-start.22 = (bf16[4,3,32,1024]{3,2,1,0:T(8,128)(2,1)}, bf16[4,3,32,1024]{3,2,1,0:T(8,128)(2,1)S(1)}, u32[]{:S(2)}) copy-start(bf16[4,3,32,1024]{3,2,1,0:T(8,128)(2,1)S(1)} %collective-permute-done.15.refs_7_) | copy-start | bytes 2359300
  561.8 5.9 collective-permute-start.17
  561.9 14.3 %collective-permute-start.16 = (bf16[4,2,32,1024]{3,2,1,0:T(8,128)(2,1)S(1)}, bf16[4,2,32,1024]{3,2,1,0:T(8,128)(2,1)S(1)}, u32[]{:S(2)}, u32[]{:S(2)}) collective-permute-start(bf16[4,2,32,1024]{3,2,1,0:T(8,128)(2,1)S(1)} %copy-done.31), channel_id=1, source_target_pairs={{0,16},{16,0},{1,17},{17,1},{2,18},{18,2},{3,19},{19,3},{4,20},{20... | collective-permute-start | bytes 1572872 | tf_op jit(solution)/shard_map/ppermute | solution.py:1219
  567.8 1.7 copy-start.4
  577.1 5.4 copy-start.30
  577.1 6.8 copy-start.23
  582.4 85.4 %reduce-scatter.8.cloned.1.call-start = ((), (), s32[]{:S(2)}) async-start(), calls=%async_computation.5 | async-start | bytes 1966080 | tf_op jit(solution)/shard_map/reduce_scatter | solution.py:1414
  582.5 24.8 %collective-permute-start.19 = (bf16[2,4,2,32,1024]{4,3,2,1,0:T(8,128)(2,1)S(1)}, bf16[2,4,2,32,1024]{4,3,2,1,0:T(8,128)(2,1)S(1)}, u32[]{:S(2)}, u32[]{:S(2)}) collective-permute-start(bf16[2,4,2,32,1024]{4,3,2,1,0:T(8,128)(2,1)S(1)} %copy-done.30), channel_id=1, source_target_pairs={{0,2},{1,3},{2,0},{3,1},{4,6},{5,7},{6,4},{7,5},{8,10},{9,11},{10,... | collective-permute-start | bytes 3145736 | tf_op jit(solution)/shard_map/ppermute | solution.py:1223
  583.9 21.7 %collective-permute-start.18 = (bf16[8,32,1024]{2,1,0:T(8,128)(2,1)S(1)}, bf16[8,32,1024]{2,1,0:T(8,128)(2,1)S(1)}, u32[]{:S(2)}, u32[]{:S(2)}) collective-permute-start(bf16[8,32,1024]{2,1,0:T(8,128)(2,1)S(1)} %bitcast.140), channel_id=1, source_target_pairs={{0,16},{16,0},{1,17},{17,1},{2,18},{18,2},{3,19},{19,3},{4,20},{20... | collective-permute-start | bytes 1572872 | tf_op jit(solution)/shard_map/ppermute | solution.py:1219
  607.2 12.9 %copy-start.19 = (bf16[2,4,2,32,1024]{4,3,2,1,0:T(8,128)(2,1)}, bf16[2,4,2,32,1024]{4,3,2,1,0:T(8,128)(2,1)S(1)}, u32[]{:S(2)}) copy-start(bf16[2,4,2,32,1024]{4,3,2,1,0:T(8,128)(2,1)S(1)} %collective-permute-done.19.refs_0_) | copy-start | bytes 3145732
  607.2 12.9 %collective-permute-start.20 = (bf16[2,4,1,32,1024]{4,3,2,1,0:T(8,128)(2,1)}, bf16[2,4,1,32,1024]{4,3,2,1,0:T(8,128)(2,1)S(1)}, u32[]{:S(2)}, u32[]{:S(2)}) collective-permute-start(bf16[2,4,1,32,1024]{4,3,2,1,0:T(8,128)(2,1)} %get-tuple-element.250), channel_id=1, source_target_pairs={{0,2},{1,3},{2,0},{3,1},{4,6},{5,7},{6,4},{7,5},{8,10},{9,11},{10,... | collective-permute-start | bytes 1572872 | tf_op jit(solution)/shard_map/ppermute | solution.py:1223
  610.2 35.2 %collective-permute-start.26 = (bf16[768,1024]{1,0:T(8,128)(2,1)}, bf16[768,1024]{1,0:T(8,128)(2,1)}, u32[]{:S(2)}, u32[]{:S(2)}) collective-permute-start(bf16[768,1024]{1,0:T(8,128)(2,1)} %get-tuple-element.263), channel_id=1, source_target_pairs={{0,16},{16,0},{1,17},{17,1},{2,18},{18,2},{3,19},{19,3},{4,20},{20... | collective-permute-start | bytes 4718600 | tf_op jit(solution)/shard_map/ppermute | solution.py:1219
  626.7 22.2 %collective-permute-start.21 = (f32[6,1024]{1,0:T(8,128)S(1)}, f32[6,1024]{1,0:T(8,128)S(1)}, u32[]{:S(2)}, u32[]{:S(2)}) collective-permute-start(f32[6,1024]{1,0:T(8,128)S(1)} %pad_maximum_fusion.6), channel_id=1, source_target_pairs={{0,1},{1,0},{2,3},{3,2},{4,5},{5,4},{6,7},{7,6},{8,9},{9,8},{10,11... | collective-permute-start | bytes 73736 | tf_op jit(solution)/shard_map/ppermute | solution.py:1624
  628.4 1.2 copy-start.16
  628.4 1.5 copy-start.18
  629.9 1.4 copy-start.13
  631.3 14.0 %copy-start.14 = (bf16[768,1024]{1,0:T(8,128)(2,1)S(1)}, bf16[768,1024]{1,0:T(8,128)(2,1)}, u32[]{:S(2)}) copy-start(bf16[768,1024]{1,0:T(8,128)(2,1)} %get-tuple-element.262) | copy-start | bytes 4718596
  649.0 4.0 collective-permute-start.22
  652.9 5.9 collective-permute-start.23
  654.6 13.0 %collective-permute-start.27 = (bf16[5,32,1024]{2,1,0:T(8,128)(2,1)}, bf16[5,32,1024]{2,1,0:T(8,128)(2,1)S(1)}, u32[]{:S(2)}, u32[]{:S(2)}) collective-permute-start(bf16[5,32,1024]{2,1,0:T(8,128)(2,1)} %bitcast.144), channel_id=1, source_target_pairs={{0,16},{16,0},{1,17},{17,1},{2,18},{18,2},{3,19},{19,3},{4,20},{20... | collective-permute-start | bytes 983048 | tf_op jit(solution)/shard_map/ppermute | solution.py:1219
  655.8 4.8 copy-start.10
  655.8 4.8 copy-start.11
  658.9 4.8 collective-permute-start.24
  663.7 3.9 collective-permute-start.25
  664.6 3.0 copy-start.27
  667.8 9.8 %copy-start.26 = (bf16[1,2,3,32,1024]{4,3,2,1,0:T(8,128)(2,1)S(1)}, bf16[1,2,3,32,1024]{4,3,2,1,0:T(8,128)(2,1)}, u32[]{:S(2)}) copy-start(bf16[1,2,3,32,1024]{4,3,2,1,0:T(8,128)(2,1)} %reduce-scatter.8.cloned.1.call-done) | copy-start | bytes 1179652
  669.1 8.5 %collective-permute-start.28 = (bf16[2,3,32,1024]{3,2,1,0:T(8,128)(2,1)}, bf16[2,3,32,1024]{3,2,1,0:T(8,128)(2,1)S(1)}, u32[]{:S(2)}, u32[]{:S(2)}) collective-permute-start(bf16[2,3,32,1024]{3,2,1,0:T(8,128)(2,1)} %bitcast.142), channel_id=1, source_target_pairs={{0,16},{16,0},{1,17},{17,1},{2,18},{18,2},{3,19},{19,3},{4,20},{20... | collective-permute-start | bytes 1179656 | tf_op jit(solution)/shard_map/ppermute | solution.py:1219
  671.4 7.3 %copy-start.1 = (s32[2,1,1536]{2,1,0:T(1,128)S(1)}, s32[2,1,1536]{2,1,0:T(1,128)}, u32[]{:S(2)}) copy-start(s32[2,1,1536]{2,1,0:T(1,128)} %param.18) | copy-start | bytes 36868
  (2 other events, 1.6 us)
Sparse Core Ops, SparseCore 0:
  12.0 94.2 all-gather.4
  107.9 91.5 all-gather.6
  476.6 43.7 reduce-scatter.3
  582.5 31.5 reduce-scatter.5
  627.0 36.8 reduce-scatter.7
where the time goes:
time: 694 us; the launch traced here: 685 us
  Pallas kernels  466 us (67%)
  waiting for transfers between devices  121 us (17%)
  local copies, waits for them, and re-layouts  32.2 us (5%)
  starting transfers between devices  27.2 us (4%)
  other arithmetic  25 us (4%)
  between operations  14.5 us (2%)
    pallas_call x1, Pallas kernels, feed(): call(feed_kernel, (8,), [once((rows, MODEL), lambda t, place: (0, 0)), on...  113 us
    pallas_call x2, Pallas kernels, attend_back(): pl.pallas_call(functools.partial(attend_back_kernel, plan), grid=(model /...  95.2 us
    ppermute x14, waiting for transfers between devices, swap(): return lax.ppermute(values, 'ctx', [(0, 1), (1, 0)])  70.1 us
    pallas_call x2, Pallas kernels, attend(): pl.pallas_call(functools.partial(attend_kernel, plan), grid=(model // 128...  55.4 us
    all_gather x1, waiting for transfers between devices, whole_pack_body(): weights = lax.all_gather(attention_shard, 'fsdp', axis=0)  29.3 us
    pallas_call x1, Pallas kernels, middle(): call(middle_kernel, (after.shape[0] // width,), [by_rows(width)] * 5 + [n...  26.2 us
    pallas_call x1, Pallas kernels, after_feed(): call(after_feed_kernel, (after.shape[0] // width,), [by_rows(width)] * 5...  21.6 us
    pallas_call x1, Pallas kernels, finish(): call(finish_kernel, (base.shape[0] // width,), [pl.BlockSpec((3, width, M...  20.9 us
  transfers between devices with their start and end apart: 34, of which 17 were waited for; matrix products, arithmetic and copies ran while one was open for 6% of the time, Pallas kernels for 44%

commit v1 on v0

--- a/solution.py
+++ b/solution.py
@@ -1127,17 +1127,17 @@
 
 def project_grad(place, left, right):
     rows = left.shape[0]
-    block = (2, 2, TILE // 256, 1, 32, MODEL)
+    block = (2, 2, 4, 1, 32, MODEL)
     return call(
         project_grad_kernel,
-        (MODEL // TILE, 3),
+        (1, 3),
         [
-            pl.BlockSpec((rows, TILE), lambda t, n, place: (0, t)),
+            pl.BlockSpec((rows, MODEL), lambda t, n, place: (0, t)),
             pl.BlockSpec((1, rows, MODEL), lambda t, n, place: (n, 0, 0)),
         ],
         [pl.BlockSpec(block, lambda t, n, place: (0, 0, t, n, 0, 0))] * 2,
         [buffer_of(3)] * 2,
-        scratch=[pltpu.VMEM((TILE, rows), jnp.bfloat16)],
+        scratch=[pltpu.VMEM((MODEL, rows), jnp.bfloat16)],
         prefetch=1,
     )(place, left, right)
 
@@ -1600,19 +1600,18 @@
     lot_d[1], total_ab, *second_c = tie(lot_d[1], total_ab, *second_c)
     second_c[1] = swap(second_c[1])
     lot_d = [(lot_d[0], over_core(lot_d[1]))]
-    (first_d,) = first_sums(place, [lot_d], [[2, 1]])
-    second_c[1], *first_d = tie(second_c[1], *first_d)
+    ((first_d,),) = first_sums(place, [lot_d])
+    second_c[1], first_d = tie(second_c[1], first_d)
     third_c = third_sums(place, [lot_c], [[first_c]], [second_c])
-    grads, third_c, total_ab, *first_d = tie(grads, third_c, total_ab, *first_d)
+    grads, third_c, total_ab, first_d = tie(grads, third_c, total_ab, first_d)
     total_c, other_ab = (over_z(third_c), swap(total_ab))
-    first_d[0] = over_x(first_d[0])
+    first_d = over_x(first_d)
     tokens_own, tokens_away, sums_zero = finish(
         held, grads, halves, grad_after_self, norms, weights, width
     )
-    tokens_own, sums_zero, other_ab, *first_d = tie(tokens_own, sums_zero, other_ab, *first_d)
-    first_d[1] = over_x(first_d[1])
+    tokens_own, sums_zero, other_ab, first_d = tie(tokens_own, sums_zero, other_ab, first_d)
     tokens_other = swap(tokens_away)
-    third_d = direct_sums(place, lot_d[0], first_d)
+    third_d = direct_sums(place, lot_d[0], [first_d])
     sums_zero, other_ab, third_d, result, result_away, encoded_own, encoded_away = tie(
         sums_zero, other_ab, third_d, result, result_away, encoded_own, encoded_away
     )

time: 694 us -> 691 us (level)
  transfers between devices with their start and end apart: 34 -> 33, of which waited for: 17 -> 16; matrix products, arithmetic and copies ran while one was open for 6% -> 6% of each run, Pallas kernels for 44% -> 45%
where the time goes in v1:
time: 691 us; the launch traced here: 682 us
  Pallas kernels  465 us (67%)
  waiting for transfers between devices  119 us (17%)
  local copies, waits for them, and re-layouts  31.7 us (5%)
  starting transfers between devices  26.3 us (4%)
  other arithmetic  26.3 us (4%)
  between operations  14.5 us (2%)
    pallas_call x1, Pallas kernels, feed(): call(feed_kernel, (8,), [once((rows, MODEL), lambda t, place: (0, 0)), on...  113 us
    pallas_call x2, Pallas kernels, attend_back(): pl.pallas_call(functools.partial(attend_back_kernel, plan), grid=(model /...  95.3 us
    ppermute x14, waiting for transfers between devices, swap(): return lax.ppermute(values, 'ctx', [(0, 1), (1, 0)])  67 us
    pallas_call x2, Pallas kernels, attend(): pl.pallas_call(functools.partial(attend_kernel, plan), grid=(model // 128...  55.4 us
    all_gather x1, waiting for transfers between devices, whole_pack_body(): weights = lax.all_gather(attention_shard, 'fsdp', axis=0)  29.3 us
    pallas_call x1, Pallas kernels, middle(): call(middle_kernel, (after.shape[0] // width,), [by_rows(width)] * 5 + [n...  26.2 us
    pallas_call x1, Pallas kernels, after_feed(): call(after_feed_kernel, (after.shape[0] // width,), [by_rows(width)] * 5...  21.6 us
    pallas_call x1, Pallas kernels, finish(): call(finish_kernel, (base.shape[0] // width,), [pl.BlockSpec((3, width, M...  21 us
  transfers between devices with their start and end apart: 33, of which 16 were waited for; matrix products, arithmetic and copies ran while one was open for 6% of the time, Pallas kernels for 45%

profile of v1, /device:TPU:0, one launch (start us, length us, event | category | flops | bytes accessed | tf_op | source)
XLA Modules:
  0.0 682.5 jit_solution(7701751155686568994)
XLA Ops:
  7.3 1.5 fusion.8.refs_7_
  8.7 3.1 shard_map.246
  13.0 3.0 collective-permute-start.1
  15.9 3.4 dynamic-slice_bitcast_fusion.3
  20.5 4.5 dynamic-slice_bitcast_fusion
  27.3 12.9 %collective-permute-done.1 = bf16[512,1024]{1,0:T(8,128)(2,1)} collective-permute-done((bf16[512,1024]{1,0:T(8,128)(2,1)}, bf16[512,1024]{1,0:T(8,128)(2,1)}, u32[]{:S(2)}, u32[]{:S(2)}) %collective-permute-start.1) | collective-permute-done | bytes 1048608 | tf_op jit(solution)/shard_map/ppermute | solution.py:1219
  40.2 1.7 bitcast_select_fusion.1
  41.9 1.5 pad_maximum_fusion.1.source_ref
  43.4 29.6 %collective-permute-done = bf16[768,1024]{1,0:T(8,128)(2,1)S(1)} collective-permute-done((bf16[768,1024]{1,0:T(8,128)(2,1)}, bf16[768,1024]{1,0:T(8,128)(2,1)S(1)}, u32[]{:S(2)}, u32[]{:S(2)}) %collective-permute-start) | collective-permute-done | bytes 1572896 | tf_op jit(solution)/shard_map/ppermute | solution.py:1219
  73.0 2.0 pad_maximum_fusion.tokens_ref
  77.0 29.3 %all-gather.5.cloned.1.call-done = bf16[8448,1024]{1,0:T(8,128)(2,1)} async-done(((bf16[528,1024]{1,0:T(8,128)(2,1)}), bf16[8448,1024]{1,0:T(8,128)(2,1)}) %all-gather.5.cloned.1.call-update) | async-done | bytes 17301520 | tf_op jit(solution)/shard_map/all_gather | solution.py:1470
  107.7 16.9 %shard_map.247 = (bf16[1536,1024]{1,0:T(8,128)(2,1)}, bf16[1536,1024]{1,0:T(8,128)(2,1)}, bf16[1536,1024]{1,0:T(8,128)(2,1)}, bf16[1536,1024]{1,0:T(8,128)(2,1)}) custom-call(s32[4]{0:T(128)} %compare_select_fusion.3.held, bf16[1536,1024]{1,0:T(8,128)(2,1)} %pad_maximum_fusion.tokens_ref, f32[8,1024]{1,0:T(8,128)} %reshape.150.norm_ref, ...), custom_call_target="tpu_custom_call" | custom-call | flops 1024 | bytes 1024 | tf_op jit(solution)/shard_map/pallas_call | solution.py:799
  124.7 1.5 collective-permute-start.2
  126.9 27.9 %shard_map.248 = (bf16[1536,1024]{1,0:T(8,128)(2,1)}, bf16[1536,1024]{1,0:T(8,128)(2,1)}) custom-call(bf16[1536,1024]{1,0:T(8,128)(2,1)} %get-tuple-element.145.q_ref, bf16[1536,1024]{1,0:T(8,128)(2,1)} %get-tuple-element.146.k_ref, bf16[1536,1024]{1,0:T(8,128)(2,1)} %get-tuple-element.147.v_ref, bf16[1536,128]{1,0:T(8,128)(2,1)} %fusion.qd_ref, ...), custom_call_target="tpu_custom_call" | custom-call | flops 1024 | bytes 1024 | tf_op jit(solution)/shard_map/pallas_call | solution.py:591
  154.7 8.4 %shard_map.250 = (bf16[1024,1024]{1,0:T(8,128)(2,1)}, bf16[1024,1024]{1,0:T(8,128)(2,1)}) custom-call(bf16[1024,1024]{1,0:T(8,128)(2,1)} %pad_maximum_fusion.1.source_ref, bf16[16,528,1024]{2,1,0:T(8,128)(2,1)} %bitcast.111, bf16[16,528,1024]{2,1,0:T(8,128)(2,1)} %bitcast.112), custom_call_target="tpu_custom_call" | custom-call | flops 1024 | bytes 1024 | tf_op jit(solution)/shard_map/pallas_call | solution.py:816
  163.1 13.4 %shard_map.249 = (f32[1536,1024]{1,0:T(8,128)}, bf16[1536,1024]{1,0:T(8,128)(2,1)}, bf16[1536,1024]{1,0:T(8,128)(2,1)}) custom-call(s32[4]{0:T(128)} %compare_select_fusion.3.held, bf16[1536,1024]{1,0:T(8,128)(2,1)} %get-tuple-element.153.mixed_ref.self_ref.out_ref, bf16[1536,1024]{1,0:T(8,128)(2,1)} %pad_maximum_fusion.tokens_ref, ...), custom_call_target="tpu_custom_call" | custom-call | flops 1024 | bytes 1024 | tf_op jit(solution)/shard_map/pallas_call | solution.py:834
  176.5 27.5 %shard_map.251 = (bf16[1536,1024]{1,0:T(8,128)(2,1)}, bf16[1536,1024]{1,0:T(8,128)(2,1)}) custom-call(bf16[1536,1024]{1,0:T(8,128)(2,1)} %get-tuple-element.154.q_ref, bf16[1024,1024]{1,0:T(8,128)(2,1)} %get-tuple-element.156.k_ref, bf16[1024,1024]{1,0:T(8,128)(2,1)} %get-tuple-element.157.v_ref, bf16[1536,128]{1,0:T(8,128)(2,1)} %fusion.qd_ref, ...), custom_call_target="tpu_custom_call" | custom-call | flops 1024 | bytes 1024 | tf_op jit(solution)/shard_map/pallas_call | solution.py:591
  204.1 1.2 copy-done.12
  205.2 13.9 %shard_map.252 = (f32[1536,1024]{1,0:T(8,128)}, bf16[1536,1024]{1,0:T(8,128)(2,1)}, bf16[1536,1024]{1,0:T(8,128)(2,1)}) custom-call(s32[4]{0:T(128)} %compare_select_fusion.3.held, bf16[1536,1024]{1,0:T(8,128)(2,1)} %get-tuple-element.160.mixed_ref.cross_ref.out_ref, f32[1536,1024]{1,0:T(8,128)} %get-tuple-element.161.base_ref.after_ref, ...), custom_call_target="tpu_custom_call" | custom-call | flops 1024 | bytes 1024 | tf_op jit(solution)/shard_map/pallas_call | solution.py:862
  219.1 113.3 %shard_map.253 = (f32[1536,1024]{1,0:T(8,128)}, f32[1536,1024]{1,0:T(8,128)}, bf16[2,2,4,4,32,1024]{5,4,3,2,1,0:T(8,128)(2,1)}, bf16[2,2,4,4,32,1024]{5,4,3,2,1,...) custom-call(s32[4]{0:T(128)} %pad_add_fusion.place_ref.place, ...), custom_call_target="tpu_custom_call" | custom-call | flops 1024 | bytes 1024 | tf_op jit(solution)/shard_map/pallas_call | solution.py:983
  332.9 21.6 %shard_map.254 = (bf16[768,1024]{1,0:T(8,128)(2,1)}, bf16[768,1024]{1,0:T(8,128)(2,1)}, f32[1536,1024]{1,0:T(8,128)}, bf16[1536,1024]{1,0:T(8,128)(2,1)}, f32[8,...) custom-call(s32[4]{0:T(128)} %compare_select_fusion.3.held, ...), custom_call_target="tpu_custom_call" | custom-call | flops 1024 | bytes 1024 | tf_op jit(solution)/shard_map/pallas_call | solution.py:1063
  354.6 1.9 copy-done.2
  356.5 6.7 shard_map.255
  363.1 1.4 collective-permute-start.6
  365.3 45.4 %shard_map.256 = (bf16[1536,1024]{1,0:T(8,128)(2,1)}, bf16[2,1024,1024]{2,1,0:T(8,128)(2,1)}) custom-call(bf16[1536,1024]{1,0:T(8,128)(2,1)} %get-tuple-element.154.q_ref, bf16[1024,1024]{1,0:T(8,128)(2,1)} %get-tuple-element.156.k_ref, bf16[1024,1024]{1,0:T(8,128)(2,1)} %get-tuple-element.157.v_ref, bf16[1536,1024]{1,0:T(8,128)(2,1)} %get-tuple-element.159.extra_ref, ...), custom_call_target="tpu_custom_call" | custom-call | flops 1024 | bytes 1024 | tf_op jit(solution)/shard_map/pallas_call | solution.py:613
  412.0 17.2 %shard_map.257 = (bf16[512,1024]{1,0:T(8,128)(2,1)}, bf16[512,1024]{1,0:T(8,128)(2,1)}, bf16[2,2,4,2,32,1024]{5,4,3,2,1,0:T(8,128)(2,1)}, bf16[2,2,4,2,32,1024]{5,4,3,2,1,0:T(8,128)(2,1)}) custom-call(s32[4]{0:T(128)} %pad_add_fusion.place_ref.place, bf16[2,1024,1024]{2,1,0:T(8,128)(2,1)} %get-tuple-element.184.grads_ref, ...), custom_call_target="tpu_custom_call" | custom-call | flops 1024 | bytes 1024 | tf_op jit(solution)/shard_map/pallas_call | solution.py:1198
  429.3 5.4 shard_map.258
  436.1 26.2 %shard_map.259 = (f32[1536,1024]{1,0:T(8,128)}, bf16[1536,1024]{1,0:T(8,128)(2,1)}, f32[8,1024]{1,0:T(8,128)}, bf16[2,2,4,2,32,1024]{5,4,3,2,1,0:T(8,128)(2,1)}, bf16[2,2,4,2,32,1024]{5,4,3,2,1,0:T(8,128)(2,1)}) custom-call(s32[4]{0:T(128)} %pad_add_fusion.place_ref.place, bf16[1536,1024]{1,0:T(8,128)(2,1)} %get-tuple-element.190.grad_ref, ...), custom_call_target="tpu_custom_call" | custom-call | flops 1024 | bytes 1024 | tf_op jit(solution)/shard_map/pallas_call | solution.py:1107
  463.6 6.1 shard_map.261
  469.9 1.2 copy-done.3
  471.1 5.4 shard_map.260
  476.6 1.5 collective-permute-start.12
  478.1 1.2 collective-permute-start.13
  480.1 49.9 %shard_map.262.right_ref.grads_ref = bf16[3,1536,1024]{2,1,0:T(8,128)(2,1)} custom-call(bf16[1536,1024]{1,0:T(8,128)(2,1)} %get-tuple-element.145.q_ref, bf16[1536,1024]{1,0:T(8,128)(2,1)} %get-tuple-element.146.k_ref, bf16[1536,1024]{1,0:T(8,128)(2,1)} %get-tuple-element.147.v_ref, bf16[1536,1024]{1,0:T(8,128)(2,1)} %get-tuple-element.150.extra_ref, ...), custom_call_target="tpu_custom_call" | custom-call | flops 1024 | bytes 1024 | tf_op jit(solution)/shard_map/pallas_call | solution.py:613
  530.0 6.3 collective-permute-done.14
  537.4 1.5 copy-done.5
  538.8 4.8 shard_map.263
  544.6 16.6 %shard_map.264 = (bf16[2,2,4,3,32,1024]{5,4,3,2,1,0:T(8,128)(2,1)}, bf16[2,2,4,3,32,1024]{5,4,3,2,1,0:T(8,128)(2,1)}) custom-call(s32[4]{0:T(128)} %pad_add_fusion.place_ref.place, bf16[1536,1024]{1,0:T(8,128)(2,1)} %get-tuple-element.220.left_ref, bf16[3,1536,1024]{2,1,0:T(8,128)(2,1)} %shard_map.262.right_ref.grads_ref), custom_call_target="tpu_custom_call" | custom-call | flops 1024 | bytes 1024 | tf_op jit(solution)/shard_map/pallas_call | solution.py:1131
  562.4 5.1 collective-permute-done.17.refs_1_.core_ref
  567.5 1.7 copy-done.4
  569.2 4.0 shard_map.265
  573.2 3.1 collective-permute-done.16.refs_8_
  576.3 5.2 shard_map.266
  584.6 21.0 %shard_map.267 = (bf16[768,1024]{1,0:T(8,128)(2,1)}, bf16[768,1024]{1,0:T(8,128)(2,1)}, f32[8,1024]{1,0:T(8,128)}) custom-call(s32[4]{0:T(128)} %compare_select_fusion.3.held, bf16[3,1536,1024]{2,1,0:T(8,128)(2,1)} %shard_map.262.right_ref.grads_ref, bf16[1536,1024]{1,0:T(8,128)(2,1)} %pad_maximum_fusion.tokens_ref, ...), custom_call_target="tpu_custom_call" | custom-call | flops 1024 | bytes 1024 | tf_op jit(solution)/shard_map/pallas_call | solution.py:1156
  605.6 1.2 collective-permute-start.25
  606.8 10.8 %collective-permute-done.19.refs_0_ = bf16[2,4,3,32,1024]{4,3,2,1,0:T(8,128)(2,1)S(1)} collective-permute-done((bf16[2,4,3,32,1024]{4,3,2,1,0:T(8,128)(2,1)S(1)}, bf16[2,4,3,32,1024]{4,3,2,1,0:T(8,128)(2,1)S(1)}, u32[]{:S(2)}, u32[]{:S(2)}) %collective-permute-start.19) | collective-permute-done | bytes 1572896 | tf_op jit(solution)/shard_map/ppermute | solution.py:1223
  618.8 5.2 shard_map.268
  626.1 1.2 fusion.12
  629.1 1.3 copy-done.14
  630.4 2.0 select_bitcast_fusion.3
  632.3 9.0 %collective-permute-done.25 = bf16[768,1024]{1,0:T(8,128)(2,1)} collective-permute-done((bf16[768,1024]{1,0:T(8,128)(2,1)}, bf16[768,1024]{1,0:T(8,128)(2,1)}, u32[]{:S(2)}, u32[]{:S(2)}) %collective-permute-start.25) | collective-permute-done | bytes 1572896 | tf_op jit(solution)/shard_map/ppermute | solution.py:1219
  641.4 1.6 select_bitcast_fusion.1
  643.0 1.9 maximum_bitcast_fusion.1
  645.0 1.4 collective-permute-start.21
  646.4 1.9 maximum_bitcast_fusion
  649.0 1.5 collective-permute-start.22
  651.5 1.5 maximum_bitcast_fusion.2
  653.0 1.8 collective-permute-done.22
  654.9 1.6 collective-permute-start.23
  657.5 3.5 collective-permute-done.23
  661.0 1.4 collective-permute-start.24
  663.3 1.8 reshape.146
  666.6 1.2 collective-permute-start.27
  670.0 4.6 collective-permute-done.27
  (155 shorter events, 35.0 us)
Async XLA Ops:
  7.2 68.4 %copy-start = (s32[2,1,1536]{2,1,0:T(1,128)S(1)}, s32[2,1,1536]{2,1,0:T(1,128)}, u32[]{:S(2)}) copy-start(s32[2,1,1536]{2,1,0:T(1,128)} %param.18) | copy-start | bytes 36868
  7.2 4.7 copy-start.9
  7.2 99.0 %all-gather.5.cloned.1.call-start = ((), (), s32[]{:S(2)}) async-start(), calls=%async_computation.6 | async-start | bytes 18382848 | tf_op jit(solution)/shard_map/all_gather | solution.py:1470
  11.9 207.2 %all-gather.7.cloned.1.call-start = ((), (), s32[]{:S(2)}) async-start(), calls=%async_computation.7 | async-start | bytes 18382848 | tf_op jit(solution)/shard_map/all_gather | solution.py:1505
  13.0 27.3 %collective-permute-start.1 = (bf16[512,1024]{1,0:T(8,128)(2,1)}, bf16[512,1024]{1,0:T(8,128)(2,1)}, u32[]{:S(2)}, u32[]{:S(2)}) collective-permute-start(bf16[512,1024]{1,0:T(8,128)(2,1)} %dynamic-slice_bitcast_fusion.4), channel_id=1, source_target_pairs={{0,16},{16,0},{1,17},{17,1},{2,18},{18,2},{3,19},{19,3},{4,20},{20... | collective-permute-start | bytes 3145736 | tf_op jit(solution)/shard_map/ppermute | solution.py:1219
  15.9 3.4 copy-start.27
  15.9 3.4 copy-start.28
  19.3 53.7 %collective-permute-start = (bf16[768,1024]{1,0:T(8,128)(2,1)}, bf16[768,1024]{1,0:T(8,128)(2,1)S(1)}, u32[]{:S(2)}, u32[]{:S(2)}) collective-permute-start(bf16[768,1024]{1,0:T(8,128)(2,1)} %get-tuple-element.339), channel_id=1, source_target_pairs={{0,16},{16,0},{1,17},{17,1},{2,18},{18,2},{3,19},{19,3},{4,20},{20... | collective-permute-start | bytes 4718600 | tf_op jit(solution)/shard_map/ppermute | solution.py:1219
  75.0 462.4 %reduce-scatter.4.cloned.1.call-start = ((), (), s32[]{:S(2)}) async-start(), calls=%async_computation.3 | async-start | bytes 2621440 | tf_op jit(solution)/shard_map/reduce_scatter | solution.py:1414
  107.7 17.0 %copy-start.16 = (bf16[768,1024]{1,0:T(8,128)(2,1)S(1)}, bf16[768,1024]{1,0:T(8,128)(2,1)}, u32[]{:S(2)}) copy-start(bf16[768,1024]{1,0:T(8,128)(2,1)} %get-tuple-element.163) | copy-start | bytes 4718596
  124.7 79.4 %collective-permute-start.2 = (bf16[768,1024]{1,0:T(8,128)(2,1)S(1)}, bf16[768,1024]{1,0:T(8,128)(2,1)S(1)}, u32[]{:S(2)}, u32[]{:S(2)}) collective-permute-start(bf16[768,1024]{1,0:T(8,128)(2,1)S(1)} %copy-done.16), channel_id=1, source_target_pairs={{0,16},{16,0},{1,17},{17,1},{2,18},{18,2},{3,19},{19,3},{4,20},{20... | collective-permute-start | bytes 4718600 | tf_op jit(solution)/shard_map/ppermute | solution.py:1219
  204.1 1.2 copy-start.12
  332.4 22.1 %collective-permute-start.3 = (bf16[2,2,4,4,32,1024]{5,4,3,2,1,0:T(8,128)(2,1)}, bf16[2,2,4,4,32,1024]{5,4,3,2,1,0:T(8,128)(2,1)S(1)}, u32[]{:S(2)}, u32[]{:S(2)}) collective-permute-start(bf16[2,2,4,4,32,1024]{5,4,3,2,1,0:T(8,128)(2,1)} %get-tuple-element.173), channel_id=1, source_target_pairs={{0,1},{1,0},{2,3},{3,2},{4,5},{5,4},{6,7},{7,6},{8,9},{9,8},{10,11... | collective-permute-start | bytes 12582920 | tf_op jit(solution)/shard_map/ppermute | solution.py:1227
  332.5 22.0 %collective-permute-start.4 = (bf16[2,2,4,4,32,1024]{5,4,3,2,1,0:T(8,128)(2,1)}, bf16[2,2,4,4,32,1024]{5,4,3,2,1,0:T(8,128)(2,1)}, u32[]{:S(2)}, u32[]{:S(2)}) collective-permute-start(bf16[2,2,4,4,32,1024]{5,4,3,2,1,0:T(8,128)(2,1)} %get-tuple-element.175), channel_id=1, source_target_pairs={{0,1},{1,0},{2,3},{3,2},{4,5},{5,4},{6,7},{7,6},{8,9},{9,8},{10,11... | collective-permute-start | bytes 12582920 | tf_op jit(solution)/shard_map/ppermute | solution.py:1227
  354.5 1.9 copy-start.2
  363.1 47.9 %collective-permute-start.6 = (bf16[2,4,4,32,1024]{4,3,2,1,0:T(8,128)(2,1)}, bf16[2,4,4,32,1024]{4,3,2,1,0:T(8,128)(2,1)S(1)}, u32[]{:S(2)}, u32[]{:S(2)}) collective-permute-start(bf16[2,4,4,32,1024]{4,3,2,1,0:T(8,128)(2,1)} %get-tuple-element.182), channel_id=1, source_target_pairs={{0,2},{1,3},{2,0},{3,1},{4,6},{5,7},{6,4},{7,5},{8,10},{9,11},{10,... | collective-permute-start | bytes 6291464 | tf_op jit(solution)/shard_map/ppermute | solution.py:1223
  364.5 47.5 %collective-permute-start.7 = (bf16[2,4,4,32,1024]{4,3,2,1,0:T(8,128)(2,1)}, bf16[2,4,4,32,1024]{4,3,2,1,0:T(8,128)(2,1)S(1)}, u32[]{:S(2)}, u32[]{:S(2)}) collective-permute-start(bf16[2,4,4,32,1024]{4,3,2,1,0:T(8,128)(2,1)} %get-tuple-element.183), channel_id=1, source_target_pairs={{0,16},{16,0},{1,17},{17,1},{2,18},{18,2},{3,19},{19,3},{4,20},{20... | collective-permute-start | bytes 6291464 | tf_op jit(solution)/shard_map/ppermute | solution.py:1219
  365.3 45.4 %collective-permute-start.5 = (bf16[2,2,4,1,32,1024]{5,4,3,2,1,0:T(8,128)(2,1)}, bf16[2,2,4,1,32,1024]{5,4,3,2,1,0:T(8,128)(2,1)S(1)}, u32[]{:S(2)}, u32[]{:S(2)}) collective-permute-start(bf16[2,2,4,1,32,1024]{5,4,3,2,1,0:T(8,128)(2,1)} %get-tuple-element.181), channel_id=1, source_target_pairs={{0,1},{1,0},{2,3},{3,2},{4,5},{5,4},{6,7},{7,6},{8,9},{9,8},{10,11... | collective-permute-start | bytes 3145736 | tf_op jit(solution)/shard_map/ppermute | solution.py:1227
  410.7 18.6 %copy-start.6 = (bf16[2,2,4,1,32,1024]{5,4,3,2,1,0:T(8,128)(2,1)}, bf16[2,2,4,1,32,1024]{5,4,3,2,1,0:T(8,128)(2,1)S(1)}, u32[]{:S(2)}) copy-start(bf16[2,2,4,1,32,1024]{5,4,3,2,1,0:T(8,128)(2,1)S(1)} %collective-permute-done.5.refs_1_) | copy-start | bytes 3145732
  411.0 18.3 %copy-start.7 = (bf16[2,4,4,32,1024]{4,3,2,1,0:T(8,128)(2,1)}, bf16[2,4,4,32,1024]{4,3,2,1,0:T(8,128)(2,1)S(1)}, u32[]{:S(2)}) copy-start(bf16[2,4,4,32,1024]{4,3,2,1,0:T(8,128)(2,1)S(1)} %collective-permute-done.6.refs_2_) | copy-start | bytes 6291460
  412.0 17.3 %copy-start.8 = (bf16[2,4,4,32,1024]{4,3,2,1,0:T(8,128)(2,1)}, bf16[2,4,4,32,1024]{4,3,2,1,0:T(8,128)(2,1)S(1)}, u32[]{:S(2)}) copy-start(bf16[2,4,4,32,1024]{4,3,2,1,0:T(8,128)(2,1)S(1)} %collective-permute-done.7.refs_5_.refs_6_) | copy-start | bytes 6291460
  434.7 27.7 %collective-permute-start.8 = (bf16[4,4,32,1024]{3,2,1,0:T(8,128)(2,1)}, bf16[4,4,32,1024]{3,2,1,0:T(8,128)(2,1)S(1)}, u32[]{:S(2)}, u32[]{:S(2)}) collective-permute-start(bf16[4,4,32,1024]{3,2,1,0:T(8,128)(2,1)} %get-tuple-element.196), channel_id=1, source_target_pairs={{0,16},{16,0},{1,17},{17,1},{2,18},{18,2},{3,19},{19,3},{4,20},{20... | collective-permute-start | bytes 3145736 | tf_op jit(solution)/shard_map/ppermute | solution.py:1219
  435.5 26.9 %collective-permute-start.9 = (bf16[4,4,32,1024]{3,2,1,0:T(8,128)(2,1)}, bf16[4,4,32,1024]{3,2,1,0:T(8,128)(2,1)S(1)}, u32[]{:S(2)}, u32[]{:S(2)}) collective-permute-start(bf16[4,4,32,1024]{3,2,1,0:T(8,128)(2,1)} %get-tuple-element.197), channel_id=1, source_target_pairs={{0,2},{1,3},{2,0},{3,1},{4,6},{5,7},{6,4},{7,5},{8,10},{9,11},{10,... | collective-permute-start | bytes 3145736 | tf_op jit(solution)/shard_map/ppermute | solution.py:1223
  462.3 1.0 copy-start.21
  462.3 1.3 copy-start.22
  462.4 7.4 %collective-permute-start.10 = (bf16[2,2,4,2,32,1024]{5,4,3,2,1,0:T(8,128)(2,1)}, bf16[2,2,4,2,32,1024]{5,4,3,2,1,0:T(8,128)(2,1)S(1)}, u32[]{:S(2)}, u32[]{:S(2)}) collective-permute-start(bf16[2,2,4,2,32,1024]{5,4,3,2,1,0:T(8,128)(2,1)} %get-tuple-element.202), channel_id=1, source_target_pairs={{0,1},{1,0},{2,3},{3,2},{4,5},{5,4},{6,7},{7,6},{8,9},{9,8},{10,11... | collective-permute-start | bytes 6291464 | tf_op jit(solution)/shard_map/ppermute | solution.py:1227
  462.4 7.5 %collective-permute-start.11 = (bf16[2,2,4,2,32,1024]{5,4,3,2,1,0:T(8,128)(2,1)}, bf16[2,2,4,2,32,1024]{5,4,3,2,1,0:T(8,128)(2,1)}, u32[]{:S(2)}, u32[]{:S(2)}) collective-permute-start(bf16[2,2,4,2,32,1024]{5,4,3,2,1,0:T(8,128)(2,1)} %get-tuple-element.204), channel_id=1, source_target_pairs={{0,1},{1,0},{2,3},{3,2},{4,5},{5,4},{6,7},{7,6},{8,9},{9,8},{10,11... | collective-permute-start | bytes 6291464 | tf_op jit(solution)/shard_map/ppermute | solution.py:1227
  469.8 1.3 copy-start.3
  476.5 173.9 %reduce-scatter.6.cloned.1.call-start = ((), (), s32[]{:S(2)}) async-start(), calls=%async_computation.4 | async-start | bytes 1638400 | tf_op jit(solution)/shard_map/reduce_scatter | solution.py:1414
  476.6 60.7 %collective-permute-start.12 = (bf16[2,4,5,32,1024]{4,3,2,1,0:T(8,128)(2,1)}, bf16[2,4,5,32,1024]{4,3,2,1,0:T(8,128)(2,1)S(1)}, u32[]{:S(2)}, u32[]{:S(2)}) collective-permute-start(bf16[2,4,5,32,1024]{4,3,2,1,0:T(8,128)(2,1)} %shard_map.260), channel_id=1, source_target_pairs={{0,2},{1,3},{2,0},{3,1},{4,6},{5,7},{6,4},{7,5},{8,10},{9,11},{10,... | collective-permute-start | bytes 7864328 | tf_op jit(solution)/shard_map/ppermute | solution.py:1223
  478.1 59.2 %collective-permute-start.13 = (bf16[768,1024]{1,0:T(8,128)(2,1)}, bf16[768,1024]{1,0:T(8,128)(2,1)}, u32[]{:S(2)}, u32[]{:S(2)}) collective-permute-start(bf16[768,1024]{1,0:T(8,128)(2,1)} %get-tuple-element.211), channel_id=1, source_target_pairs={{0,16},{16,0},{1,17},{17,1},{2,18},{18,2},{3,19},{19,3},{4,20},{20... | collective-permute-start | bytes 4718600 | tf_op jit(solution)/shard_map/ppermute | solution.py:1219
  479.3 57.1 %collective-permute-start.14 = (bf16[512,1024]{1,0:T(8,128)(2,1)}, bf16[512,1024]{1,0:T(8,128)(2,1)S(1)}, u32[]{:S(2)}, u32[]{:S(2)}) collective-permute-start(bf16[512,1024]{1,0:T(8,128)(2,1)} %get-tuple-element.212), channel_id=1, source_target_pairs={{0,16},{16,0},{1,17},{17,1},{2,18},{18,2},{3,19},{19,3},{4,20},{20... | collective-permute-start | bytes 3145736 | tf_op jit(solution)/shard_map/ppermute | solution.py:1219
  536.4 1.0 copy-start.19
  537.3 1.5 copy-start.5
  543.6 18.0 %collective-permute-start.15 = (bf16[4,3,32,1024]{3,2,1,0:T(8,128)(2,1)}, bf16[4,3,32,1024]{3,2,1,0:T(8,128)(2,1)S(1)}, u32[]{:S(2)}, u32[]{:S(2)}) collective-permute-start(bf16[4,3,32,1024]{3,2,1,0:T(8,128)(2,1)} %get-tuple-element.223), channel_id=1, source_target_pairs={{0,16},{16,0},{1,17},{17,1},{2,18},{18,2},{3,19},{19,3},{4,20},{20... | collective-permute-start | bytes 2359304 | tf_op jit(solution)/shard_map/ppermute | solution.py:1219
  561.6 14.7 %copy-start.23 = (bf16[4,3,32,1024]{3,2,1,0:T(8,128)(2,1)}, bf16[4,3,32,1024]{3,2,1,0:T(8,128)(2,1)S(1)}, u32[]{:S(2)}) copy-start(bf16[4,3,32,1024]{3,2,1,0:T(8,128)(2,1)S(1)} %collective-permute-done.15.refs_7_) | copy-start | bytes 2359300
  561.6 5.9 collective-permute-start.17
  561.6 14.7 %collective-permute-start.16 = (bf16[4,2,32,1024]{3,2,1,0:T(8,128)(2,1)}, bf16[4,2,32,1024]{3,2,1,0:T(8,128)(2,1)}, u32[]{:S(2)}, u32[]{:S(2)}) collective-permute-start(bf16[4,2,32,1024]{3,2,1,0:T(8,128)(2,1)} %get-tuple-element.226), channel_id=1, source_target_pairs={{0,16},{16,0},{1,17},{17,1},{2,18},{18,2},{3,19},{19,3},{4,20},{20... | collective-permute-start | bytes 1572872 | tf_op jit(solution)/shard_map/ppermute | solution.py:1219
  567.5 1.7 copy-start.4
  573.2 8.3 %copy-start.17 = (bf16[2,4,3,32,1024]{4,3,2,1,0:T(8,128)(2,1)S(1)}, bf16[2,4,3,32,1024]{4,3,2,1,0:T(8,128)(2,1)}, u32[]{:S(2)}) copy-start(bf16[2,4,3,32,1024]{4,3,2,1,0:T(8,128)(2,1)} %shard_map.265) | copy-start | bytes 4718596
  581.5 83.8 %reduce-scatter.8.cloned.1.call-start = ((), (), s32[]{:S(2)}) async-start(), calls=%async_computation.5 | async-start | bytes 1966080 | tf_op jit(solution)/shard_map/reduce_scatter | solution.py:1414
  581.6 36.1 %collective-permute-start.19 = (bf16[2,4,3,32,1024]{4,3,2,1,0:T(8,128)(2,1)S(1)}, bf16[2,4,3,32,1024]{4,3,2,1,0:T(8,128)(2,1)S(1)}, u32[]{:S(2)}, u32[]{:S(2)}) collective-permute-start(bf16[2,4,3,32,1024]{4,3,2,1,0:T(8,128)(2,1)S(1)} %copy-done.17), channel_id=1, source_target_pairs={{0,2},{1,3},{2,0},{3,1},{4,6},{5,7},{6,4},{7,5},{8,10},{9,11},{10,... | collective-permute-start | bytes 4718600 | tf_op jit(solution)/shard_map/ppermute | solution.py:1223
  582.3 24.5 %collective-permute-start.18 = (bf16[8,32,1024]{2,1,0:T(8,128)(2,1)}, bf16[8,32,1024]{2,1,0:T(8,128)(2,1)}, u32[]{:S(2)}, u32[]{:S(2)}) collective-permute-start(bf16[8,32,1024]{2,1,0:T(8,128)(2,1)} %bitcast.140), channel_id=1, source_target_pairs={{0,16},{16,0},{1,17},{17,1},{2,18},{18,2},{3,19},{19,3},{4,20},{20... | collective-permute-start | bytes 1572872 | tf_op jit(solution)/shard_map/ppermute | solution.py:1219
  605.6 35.8 %collective-permute-start.25 = (bf16[768,1024]{1,0:T(8,128)(2,1)}, bf16[768,1024]{1,0:T(8,128)(2,1)}, u32[]{:S(2)}, u32[]{:S(2)}) collective-permute-start(bf16[768,1024]{1,0:T(8,128)(2,1)} %get-tuple-element.253), channel_id=1, source_target_pairs={{0,16},{16,0},{1,17},{17,1},{2,18},{18,2},{3,19},{19,3},{4,20},{20... | collective-permute-start | bytes 4718600 | tf_op jit(solution)/shard_map/ppermute | solution.py:1219
  617.6 1.1 copy-start.13
  618.8 6.0 copy-start.24
  624.7 20.2 %collective-permute-start.20 = (f32[6,1024]{1,0:T(8,128)S(1)}, f32[6,1024]{1,0:T(8,128)S(1)}, u32[]{:S(2)}, u32[]{:S(2)}) collective-permute-start(f32[6,1024]{1,0:T(8,128)S(1)} %pad_maximum_fusion.6), channel_id=1, source_target_pairs={{0,1},{1,0},{2,3},{3,2},{4,5},{5,4},{6,7},{7,6},{8,9},{9,8},{10,11... | collective-permute-start | bytes 73736 | tf_op jit(solution)/shard_map/ppermute | solution.py:1623
  627.4 1.2 copy-start.18
  627.4 1.5 copy-start.20
  629.0 1.4 copy-start.14
  630.4 11.0 %copy-start.15 = (bf16[768,1024]{1,0:T(8,128)(2,1)S(1)}, bf16[768,1024]{1,0:T(8,128)(2,1)}, u32[]{:S(2)}) copy-start(bf16[768,1024]{1,0:T(8,128)(2,1)} %get-tuple-element.252) | copy-start | bytes 4718596
  645.0 4.0 collective-permute-start.21
  649.0 5.9 collective-permute-start.22
  650.4 14.7 %collective-permute-start.26 = (bf16[5,32,1024]{2,1,0:T(8,128)(2,1)}, bf16[5,32,1024]{2,1,0:T(8,128)(2,1)S(1)}, u32[]{:S(2)}, u32[]{:S(2)}) collective-permute-start(bf16[5,32,1024]{2,1,0:T(8,128)(2,1)} %bitcast.144), channel_id=1, source_target_pairs={{0,16},{16,0},{1,17},{17,1},{2,18},{18,2},{3,19},{19,3},{4,20},{20... | collective-permute-start | bytes 983048 | tf_op jit(solution)/shard_map/ppermute | solution.py:1219
  651.5 5.0 copy-start.10
  651.5 5.0 copy-start.11
  654.9 6.1 collective-permute-start.23
  661.0 4.1 collective-permute-start.24
  662.5 2.7 copy-start.26
  665.4 9.2 %copy-start.25 = (bf16[1,2,3,32,1024]{4,3,2,1,0:T(8,128)(2,1)S(1)}, bf16[1,2,3,32,1024]{4,3,2,1,0:T(8,128)(2,1)}, u32[]{:S(2)}) copy-start(bf16[1,2,3,32,1024]{4,3,2,1,0:T(8,128)(2,1)} %reduce-scatter.8.cloned.1.call-done) | copy-start | bytes 1179652
  666.6 8.0 %collective-permute-start.27 = (bf16[2,3,32,1024]{3,2,1,0:T(8,128)(2,1)}, bf16[2,3,32,1024]{3,2,1,0:T(8,128)(2,1)S(1)}, u32[]{:S(2)}, u32[]{:S(2)}) collective-permute-start(bf16[2,3,32,1024]{3,2,1,0:T(8,128)(2,1)} %bitcast.142), channel_id=1, source_target_pairs={{0,16},{16,0},{1,17},{17,1},{2,18},{18,2},{3,19},{19,3},{4,20},{20... | collective-permute-start | bytes 1179656 | tf_op jit(solution)/shard_map/ppermute | solution.py:1219
  669.2 6.5 copy-start.1
Sparse Core Ops, SparseCore 0:
  12.0 94.2 all-gather.4
  107.8 91.5 all-gather.6
  476.7 43.5 reduce-scatter.3
  581.6 30.4 reduce-scatter.5
  626.1 36.0 reduce-scatter.7

commit v2 on v1

--- a/solution.py
+++ b/solution.py
@@ -936,7 +936,7 @@
 
     win, wout = (gathered(win_ref), gathered(wout_ref))
     rows = third_ref.shape[0]
-    lots = [slice(start, start + TILE) for start in range(0, rows, TILE)]
+    lots = [slice(start, start + rows // 4) for start in range(0, rows, rows // 4)]
 
     def enter(lot):
         return (dot(third_ref[lot], win), dot(grad_ref[lot], wout, NT))

time: 691 us -> 686 us (level)
  no operation moved by 1% of the time
where the time goes in v2:
time: 686 us; the launch traced here: 682 us
  Pallas kernels  464 us (68%)
  waiting for transfers between devices  119 us (17%)
  local copies, waits for them, and re-layouts  31.7 us (5%)
  other arithmetic  26.3 us (4%)
  starting transfers between devices  26.1 us (4%)
  between operations  14.5 us (2%)
    pallas_call x1, Pallas kernels, feed(): call(feed_kernel, (8,), [once((rows, MODEL), lambda t, place: (0, 0)), on...  113 us
    pallas_call x2, Pallas kernels, attend_back(): pl.pallas_call(functools.partial(attend_back_kernel, plan), grid=(model /...  95.2 us
    ppermute x14, waiting for transfers between devices, swap(): return lax.ppermute(values, 'ctx', [(0, 1), (1, 0)])  67.3 us
    pallas_call x2, Pallas kernels, attend(): pl.pallas_call(functools.partial(attend_kernel, plan), grid=(model // 128...  55.4 us
    all_gather x1, waiting for transfers between devices, whole_pack_body(): weights = lax.all_gather(attention_shard, 'fsdp', axis=0)  29.3 us
    pallas_call x1, Pallas kernels, middle(): call(middle_kernel, (after.shape[0] // width,), [by_rows(width)] * 5 + [n...  26.2 us
    pallas_call x1, Pallas kernels, after_feed(): call(after_feed_kernel, (after.shape[0] // width,), [by_rows(width)] * 5...  21.6 us
    pallas_call x1, Pallas kernels, finish(): call(finish_kernel, (base.shape[0] // width,), [pl.BlockSpec((3, width, M...  21 us
  transfers between devices with their start and end apart: 33, of which 16 were waited for; matrix products, arithmetic and copies ran while one was open for 6% of the time, Pallas kernels for 45%

profile of v2, /device:TPU:0, one launch (start us, length us, event | category | flops | bytes accessed | tf_op | source)
XLA Modules:
  0.0 681.8 jit_solution(13969875247558761500)
XLA Ops:
  7.3 1.5 fusion.8.refs_7_
  8.7 3.1 shard_map.246
  13.0 3.0 collective-permute-start.1
  15.9 3.4 dynamic-slice_bitcast_fusion.3
  20.5 4.5 dynamic-slice_bitcast_fusion
  27.3 12.9 %collective-permute-done.1 = bf16[512,1024]{1,0:T(8,128)(2,1)} collective-permute-done((bf16[512,1024]{1,0:T(8,128)(2,1)}, bf16[512,1024]{1,0:T(8,128)(2,1)}, u32[]{:S(2)}, u32[]{:S(2)}) %collective-permute-start.1) | collective-permute-done | bytes 1048608 | tf_op jit(solution)/shard_map/ppermute | solution.py:1219
  40.2 1.7 bitcast_select_fusion.1
  41.9 1.5 pad_maximum_fusion.1.source_ref
  43.4 29.6 %collective-permute-done = bf16[768,1024]{1,0:T(8,128)(2,1)S(1)} collective-permute-done((bf16[768,1024]{1,0:T(8,128)(2,1)}, bf16[768,1024]{1,0:T(8,128)(2,1)S(1)}, u32[]{:S(2)}, u32[]{:S(2)}) %collective-permute-start) | collective-permute-done | bytes 1572896 | tf_op jit(solution)/shard_map/ppermute | solution.py:1219
  73.0 2.0 pad_maximum_fusion.tokens_ref
  77.0 29.3 %all-gather.5.cloned.1.call-done = bf16[8448,1024]{1,0:T(8,128)(2,1)} async-done(((bf16[528,1024]{1,0:T(8,128)(2,1)}), bf16[8448,1024]{1,0:T(8,128)(2,1)}) %all-gather.5.cloned.1.call-update) | async-done | bytes 17301520 | tf_op jit(solution)/shard_map/all_gather | solution.py:1470
  107.7 16.9 %shard_map.247 = (bf16[1536,1024]{1,0:T(8,128)(2,1)}, bf16[1536,1024]{1,0:T(8,128)(2,1)}, bf16[1536,1024]{1,0:T(8,128)(2,1)}, bf16[1536,1024]{1,0:T(8,128)(2,1)}) custom-call(s32[4]{0:T(128)} %compare_select_fusion.3.held, bf16[1536,1024]{1,0:T(8,128)(2,1)} %pad_maximum_fusion.tokens_ref, f32[8,1024]{1,0:T(8,128)} %reshape.150.norm_ref, ...), custom_call_target="tpu_custom_call" | custom-call | flops 1024 | bytes 1024 | tf_op jit(solution)/shard_map/pallas_call | solution.py:799
  124.7 1.5 collective-permute-start.2
  126.9 27.9 %shard_map.248 = (bf16[1536,1024]{1,0:T(8,128)(2,1)}, bf16[1536,1024]{1,0:T(8,128)(2,1)}) custom-call(bf16[1536,1024]{1,0:T(8,128)(2,1)} %get-tuple-element.145.q_ref, bf16[1536,1024]{1,0:T(8,128)(2,1)} %get-tuple-element.146.k_ref, bf16[1536,1024]{1,0:T(8,128)(2,1)} %get-tuple-element.147.v_ref, bf16[1536,128]{1,0:T(8,128)(2,1)} %fusion.qd_ref, ...), custom_call_target="tpu_custom_call" | custom-call | flops 1024 | bytes 1024 | tf_op jit(solution)/shard_map/pallas_call | solution.py:591
  154.7 8.4 %shard_map.250 = (bf16[1024,1024]{1,0:T(8,128)(2,1)}, bf16[1024,1024]{1,0:T(8,128)(2,1)}) custom-call(bf16[1024,1024]{1,0:T(8,128)(2,1)} %pad_maximum_fusion.1.source_ref, bf16[16,528,1024]{2,1,0:T(8,128)(2,1)} %bitcast.111, bf16[16,528,1024]{2,1,0:T(8,128)(2,1)} %bitcast.112), custom_call_target="tpu_custom_call" | custom-call | flops 1024 | bytes 1024 | tf_op jit(solution)/shard_map/pallas_call | solution.py:816
  163.1 13.4 %shard_map.249 = (f32[1536,1024]{1,0:T(8,128)}, bf16[1536,1024]{1,0:T(8,128)(2,1)}, bf16[1536,1024]{1,0:T(8,128)(2,1)}) custom-call(s32[4]{0:T(128)} %compare_select_fusion.3.held, bf16[1536,1024]{1,0:T(8,128)(2,1)} %get-tuple-element.153.mixed_ref.self_ref.out_ref, bf16[1536,1024]{1,0:T(8,128)(2,1)} %pad_maximum_fusion.tokens_ref, ...), custom_call_target="tpu_custom_call" | custom-call | flops 1024 | bytes 1024 | tf_op jit(solution)/shard_map/pallas_call | solution.py:834
  176.5 27.5 %shard_map.251 = (bf16[1536,1024]{1,0:T(8,128)(2,1)}, bf16[1536,1024]{1,0:T(8,128)(2,1)}) custom-call(bf16[1536,1024]{1,0:T(8,128)(2,1)} %get-tuple-element.154.q_ref, bf16[1024,1024]{1,0:T(8,128)(2,1)} %get-tuple-element.156.k_ref, bf16[1024,1024]{1,0:T(8,128)(2,1)} %get-tuple-element.157.v_ref, bf16[1536,128]{1,0:T(8,128)(2,1)} %fusion.qd_ref, ...), custom_call_target="tpu_custom_call" | custom-call | flops 1024 | bytes 1024 | tf_op jit(solution)/shard_map/pallas_call | solution.py:591
  205.2 13.7 %shard_map.252 = (f32[1536,1024]{1,0:T(8,128)}, bf16[1536,1024]{1,0:T(8,128)(2,1)}, bf16[1536,1024]{1,0:T(8,128)(2,1)}) custom-call(s32[4]{0:T(128)} %compare_select_fusion.3.held, bf16[1536,1024]{1,0:T(8,128)(2,1)} %get-tuple-element.160.mixed_ref.cross_ref.out_ref, f32[1536,1024]{1,0:T(8,128)} %get-tuple-element.161.base_ref.after_ref, ...), custom_call_target="tpu_custom_call" | custom-call | flops 1024 | bytes 1024 | tf_op jit(solution)/shard_map/pallas_call | solution.py:862
  218.9 112.6 %shard_map.253 = (f32[1536,1024]{1,0:T(8,128)}, f32[1536,1024]{1,0:T(8,128)}, bf16[2,2,4,4,32,1024]{5,4,3,2,1,0:T(8,128)(2,1)}, bf16[2,2,4,4,32,1024]{5,4,3,2,1,...) custom-call(s32[4]{0:T(128)} %pad_add_fusion.place_ref.place, ...), custom_call_target="tpu_custom_call" | custom-call | flops 1024 | bytes 1024 | tf_op jit(solution)/shard_map/pallas_call | solution.py:983
  332.0 21.6 %shard_map.254 = (bf16[768,1024]{1,0:T(8,128)(2,1)}, bf16[768,1024]{1,0:T(8,128)(2,1)}, f32[1536,1024]{1,0:T(8,128)}, bf16[1536,1024]{1,0:T(8,128)(2,1)}, f32[8,...) custom-call(s32[4]{0:T(128)} %compare_select_fusion.3.held, ...), custom_call_target="tpu_custom_call" | custom-call | flops 1024 | bytes 1024 | tf_op jit(solution)/shard_map/pallas_call | solution.py:1063
  353.6 1.9 copy-done.2
  355.6 6.7 shard_map.255
  362.2 1.4 collective-permute-start.6
  364.2 45.4 %shard_map.256 = (bf16[1536,1024]{1,0:T(8,128)(2,1)}, bf16[2,1024,1024]{2,1,0:T(8,128)(2,1)}) custom-call(bf16[1536,1024]{1,0:T(8,128)(2,1)} %get-tuple-element.154.q_ref, bf16[1024,1024]{1,0:T(8,128)(2,1)} %get-tuple-element.156.k_ref, bf16[1024,1024]{1,0:T(8,128)(2,1)} %get-tuple-element.157.v_ref, bf16[1536,1024]{1,0:T(8,128)(2,1)} %get-tuple-element.159.extra_ref, ...), custom_call_target="tpu_custom_call" | custom-call | flops 1024 | bytes 1024 | tf_op jit(solution)/shard_map/pallas_call | solution.py:613
  411.1 17.2 %shard_map.257 = (bf16[512,1024]{1,0:T(8,128)(2,1)}, bf16[512,1024]{1,0:T(8,128)(2,1)}, bf16[2,2,4,2,32,1024]{5,4,3,2,1,0:T(8,128)(2,1)}, bf16[2,2,4,2,32,1024]{5,4,3,2,1,0:T(8,128)(2,1)}) custom-call(s32[4]{0:T(128)} %pad_add_fusion.place_ref.place, bf16[2,1024,1024]{2,1,0:T(8,128)(2,1)} %get-tuple-element.184.grads_ref, ...), custom_call_target="tpu_custom_call" | custom-call | flops 1024 | bytes 1024 | tf_op jit(solution)/shard_map/pallas_call | solution.py:1198
  428.4 5.4 shard_map.258
  435.1 26.2 %shard_map.259 = (f32[1536,1024]{1,0:T(8,128)}, bf16[1536,1024]{1,0:T(8,128)(2,1)}, f32[8,1024]{1,0:T(8,128)}, bf16[2,2,4,2,32,1024]{5,4,3,2,1,0:T(8,128)(2,1)}, bf16[2,2,4,2,32,1024]{5,4,3,2,1,0:T(8,128)(2,1)}) custom-call(s32[4]{0:T(128)} %pad_add_fusion.place_ref.place, bf16[1536,1024]{1,0:T(8,128)(2,1)} %get-tuple-element.190.grad_ref, ...), custom_call_target="tpu_custom_call" | custom-call | flops 1024 | bytes 1024 | tf_op jit(solution)/shard_map/pallas_call | solution.py:1107
  462.7 6.1 shard_map.261
  469.0 1.2 copy-done.3
  470.2 5.4 shard_map.260
  475.6 1.3 collective-permute-start.12
  476.9 1.4 collective-permute-start.13
  479.0 49.8 %shard_map.262.right_ref.grads_ref = bf16[3,1536,1024]{2,1,0:T(8,128)(2,1)} custom-call(bf16[1536,1024]{1,0:T(8,128)(2,1)} %get-tuple-element.145.q_ref, bf16[1536,1024]{1,0:T(8,128)(2,1)} %get-tuple-element.146.k_ref, bf16[1536,1024]{1,0:T(8,128)(2,1)} %get-tuple-element.147.v_ref, bf16[1536,1024]{1,0:T(8,128)(2,1)} %get-tuple-element.150.extra_ref, ...), custom_call_target="tpu_custom_call" | custom-call | flops 1024 | bytes 1024 | tf_op jit(solution)/shard_map/pallas_call | solution.py:613
  528.8 6.7 collective-permute-done.14
  536.4 1.5 copy-done.5
  537.9 4.8 shard_map.263
  543.7 16.6 %shard_map.264 = (bf16[2,2,4,3,32,1024]{5,4,3,2,1,0:T(8,128)(2,1)}, bf16[2,2,4,3,32,1024]{5,4,3,2,1,0:T(8,128)(2,1)}) custom-call(s32[4]{0:T(128)} %pad_add_fusion.place_ref.place, bf16[1536,1024]{1,0:T(8,128)(2,1)} %get-tuple-element.220.left_ref, bf16[3,1536,1024]{2,1,0:T(8,128)(2,1)} %shard_map.262.right_ref.grads_ref), custom_call_target="tpu_custom_call" | custom-call | flops 1024 | bytes 1024 | tf_op jit(solution)/shard_map/pallas_call | solution.py:1131
  561.5 5.3 collective-permute-done.17.refs_1_.core_ref
  566.8 1.7 copy-done.4
  568.5 4.0 shard_map.265
  572.5 3.1 collective-permute-done.16.refs_8_
  575.6 5.2 shard_map.266
  583.7 21.0 %shard_map.267 = (bf16[768,1024]{1,0:T(8,128)(2,1)}, bf16[768,1024]{1,0:T(8,128)(2,1)}, f32[8,1024]{1,0:T(8,128)}) custom-call(s32[4]{0:T(128)} %compare_select_fusion.3.held, bf16[3,1536,1024]{2,1,0:T(8,128)(2,1)} %shard_map.262.right_ref.grads_ref, bf16[1536,1024]{1,0:T(8,128)(2,1)} %pad_maximum_fusion.tokens_ref, ...), custom_call_target="tpu_custom_call" | custom-call | flops 1024 | bytes 1024 | tf_op jit(solution)/shard_map/pallas_call | solution.py:1156
  604.6 1.3 collective-permute-start.25
  605.9 11.0 %collective-permute-done.19.refs_0_ = bf16[2,4,3,32,1024]{4,3,2,1,0:T(8,128)(2,1)S(1)} collective-permute-done((bf16[2,4,3,32,1024]{4,3,2,1,0:T(8,128)(2,1)S(1)}, bf16[2,4,3,32,1024]{4,3,2,1,0:T(8,128)(2,1)S(1)}, u32[]{:S(2)}, u32[]{:S(2)}) %collective-permute-start.19) | collective-permute-done | bytes 1572896 | tf_op jit(solution)/shard_map/ppermute | solution.py:1223
  618.1 5.2 shard_map.268
  625.4 1.2 fusion.12
  628.4 1.3 copy-done.14
  629.7 2.0 select_bitcast_fusion.3
  631.7 8.8 %collective-permute-done.25 = bf16[768,1024]{1,0:T(8,128)(2,1)} collective-permute-done((bf16[768,1024]{1,0:T(8,128)(2,1)}, bf16[768,1024]{1,0:T(8,128)(2,1)}, u32[]{:S(2)}, u32[]{:S(2)}) %collective-permute-start.25) | collective-permute-done | bytes 1572896 | tf_op jit(solution)/shard_map/ppermute | solution.py:1219
  640.4 1.6 select_bitcast_fusion.1
  642.1 1.9 maximum_bitcast_fusion.1
  644.0 1.4 collective-permute-start.21
  645.5 1.9 maximum_bitcast_fusion
  648.0 1.6 collective-permute-start.22
  649.6 1.4 collective-permute-start.26
  651.1 1.5 maximum_bitcast_fusion.2
  652.6 1.4 collective-permute-done.22
  654.0 1.7 collective-permute-start.23
  656.7 3.5 collective-permute-done.23
  660.2 1.5 collective-permute-start.24
  662.6 1.8 reshape.146
  665.9 1.2 collective-permute-start.27
  669.3 4.6 collective-permute-done.27
  (155 shorter events, 34.5 us)
Async XLA Ops:
  7.2 68.4 %copy-start = (s32[2,1,1536]{2,1,0:T(1,128)S(1)}, s32[2,1,1536]{2,1,0:T(1,128)}, u32[]{:S(2)}) copy-start(s32[2,1,1536]{2,1,0:T(1,128)} %param.18) | copy-start | bytes 36868
  7.2 4.7 copy-start.9
  7.2 99.0 %all-gather.5.cloned.1.call-start = ((), (), s32[]{:S(2)}) async-start(), calls=%async_computation.6 | async-start | bytes 18382848 | tf_op jit(solution)/shard_map/all_gather | solution.py:1470
  11.9 207.1 %all-gather.7.cloned.1.call-start = ((), (), s32[]{:S(2)}) async-start(), calls=%async_computation.7 | async-start | bytes 18382848 | tf_op jit(solution)/shard_map/all_gather | solution.py:1505
  13.0 27.3 %collective-permute-start.1 = (bf16[512,1024]{1,0:T(8,128)(2,1)}, bf16[512,1024]{1,0:T(8,128)(2,1)}, u32[]{:S(2)}, u32[]{:S(2)}) collective-permute-start(bf16[512,1024]{1,0:T(8,128)(2,1)} %dynamic-slice_bitcast_fusion.4), channel_id=1, source_target_pairs={{0,16},{16,0},{1,17},{17,1},{2,18},{18,2},{3,19},{19,3},{4,20},{20... | collective-permute-start | bytes 3145736 | tf_op jit(solution)/shard_map/ppermute | solution.py:1219
  15.9 3.4 copy-start.27
  15.9 3.4 copy-start.28
  19.3 53.7 %collective-permute-start = (bf16[768,1024]{1,0:T(8,128)(2,1)}, bf16[768,1024]{1,0:T(8,128)(2,1)S(1)}, u32[]{:S(2)}, u32[]{:S(2)}) collective-permute-start(bf16[768,1024]{1,0:T(8,128)(2,1)} %get-tuple-element.339), channel_id=1, source_target_pairs={{0,16},{16,0},{1,17},{17,1},{2,18},{18,2},{3,19},{19,3},{4,20},{20... | collective-permute-start | bytes 4718600 | tf_op jit(solution)/shard_map/ppermute | solution.py:1219
  75.0 461.4 %reduce-scatter.4.cloned.1.call-start = ((), (), s32[]{:S(2)}) async-start(), calls=%async_computation.3 | async-start | bytes 2621440 | tf_op jit(solution)/shard_map/reduce_scatter | solution.py:1414
  107.7 17.0 %copy-start.16 = (bf16[768,1024]{1,0:T(8,128)(2,1)S(1)}, bf16[768,1024]{1,0:T(8,128)(2,1)}, u32[]{:S(2)}) copy-start(bf16[768,1024]{1,0:T(8,128)(2,1)} %get-tuple-element.163) | copy-start | bytes 4718596
  124.7 79.4 %collective-permute-start.2 = (bf16[768,1024]{1,0:T(8,128)(2,1)S(1)}, bf16[768,1024]{1,0:T(8,128)(2,1)S(1)}, u32[]{:S(2)}, u32[]{:S(2)}) collective-permute-start(bf16[768,1024]{1,0:T(8,128)(2,1)S(1)} %copy-done.16), channel_id=1, source_target_pairs={{0,16},{16,0},{1,17},{17,1},{2,18},{18,2},{3,19},{19,3},{4,20},{20... | collective-permute-start | bytes 4718600 | tf_op jit(solution)/shard_map/ppermute | solution.py:1219
  204.1 1.2 copy-start.12
  331.5 22.1 %collective-permute-start.3 = (bf16[2,2,4,4,32,1024]{5,4,3,2,1,0:T(8,128)(2,1)}, bf16[2,2,4,4,32,1024]{5,4,3,2,1,0:T(8,128)(2,1)S(1)}, u32[]{:S(2)}, u32[]{:S(2)}) collective-permute-start(bf16[2,2,4,4,32,1024]{5,4,3,2,1,0:T(8,128)(2,1)} %get-tuple-element.173), channel_id=1, source_target_pairs={{0,1},{1,0},{2,3},{3,2},{4,5},{5,4},{6,7},{7,6},{8,9},{9,8},{10,11... | collective-permute-start | bytes 12582920 | tf_op jit(solution)/shard_map/ppermute | solution.py:1227
  331.5 22.1 %collective-permute-start.4 = (bf16[2,2,4,4,32,1024]{5,4,3,2,1,0:T(8,128)(2,1)}, bf16[2,2,4,4,32,1024]{5,4,3,2,1,0:T(8,128)(2,1)}, u32[]{:S(2)}, u32[]{:S(2)}) collective-permute-start(bf16[2,2,4,4,32,1024]{5,4,3,2,1,0:T(8,128)(2,1)} %get-tuple-element.175), channel_id=1, source_target_pairs={{0,1},{1,0},{2,3},{3,2},{4,5},{5,4},{6,7},{7,6},{8,9},{9,8},{10,11... | collective-permute-start | bytes 12582920 | tf_op jit(solution)/shard_map/ppermute | solution.py:1227
  353.6 1.9 copy-start.2
  362.2 47.8 %collective-permute-start.6 = (bf16[2,4,4,32,1024]{4,3,2,1,0:T(8,128)(2,1)}, bf16[2,4,4,32,1024]{4,3,2,1,0:T(8,128)(2,1)S(1)}, u32[]{:S(2)}, u32[]{:S(2)}) collective-permute-start(bf16[2,4,4,32,1024]{4,3,2,1,0:T(8,128)(2,1)} %get-tuple-element.182), channel_id=1, source_target_pairs={{0,2},{1,3},{2,0},{3,1},{4,6},{5,7},{6,4},{7,5},{8,10},{9,11},{10,... | collective-permute-start | bytes 6291464 | tf_op jit(solution)/shard_map/ppermute | solution.py:1223
  363.6 47.5 %collective-permute-start.7 = (bf16[2,4,4,32,1024]{4,3,2,1,0:T(8,128)(2,1)}, bf16[2,4,4,32,1024]{4,3,2,1,0:T(8,128)(2,1)S(1)}, u32[]{:S(2)}, u32[]{:S(2)}) collective-permute-start(bf16[2,4,4,32,1024]{4,3,2,1,0:T(8,128)(2,1)} %get-tuple-element.183), channel_id=1, source_target_pairs={{0,16},{16,0},{1,17},{17,1},{2,18},{18,2},{3,19},{19,3},{4,20},{20... | collective-permute-start | bytes 6291464 | tf_op jit(solution)/shard_map/ppermute | solution.py:1219
  364.2 45.4 %collective-permute-start.5 = (bf16[2,2,4,1,32,1024]{5,4,3,2,1,0:T(8,128)(2,1)}, bf16[2,2,4,1,32,1024]{5,4,3,2,1,0:T(8,128)(2,1)S(1)}, u32[]{:S(2)}, u32[]{:S(2)}) collective-permute-start(bf16[2,2,4,1,32,1024]{5,4,3,2,1,0:T(8,128)(2,1)} %get-tuple-element.181), channel_id=1, source_target_pairs={{0,1},{1,0},{2,3},{3,2},{4,5},{5,4},{6,7},{7,6},{8,9},{9,8},{10,11... | collective-permute-start | bytes 3145736 | tf_op jit(solution)/shard_map/ppermute | solution.py:1227
  409.6 18.8 %copy-start.6 = (bf16[2,2,4,1,32,1024]{5,4,3,2,1,0:T(8,128)(2,1)}, bf16[2,2,4,1,32,1024]{5,4,3,2,1,0:T(8,128)(2,1)S(1)}, u32[]{:S(2)}) copy-start(bf16[2,2,4,1,32,1024]{5,4,3,2,1,0:T(8,128)(2,1)S(1)} %collective-permute-done.5.refs_1_) | copy-start | bytes 3145732
  410.0 18.4 %copy-start.7 = (bf16[2,4,4,32,1024]{4,3,2,1,0:T(8,128)(2,1)}, bf16[2,4,4,32,1024]{4,3,2,1,0:T(8,128)(2,1)S(1)}, u32[]{:S(2)}) copy-start(bf16[2,4,4,32,1024]{4,3,2,1,0:T(8,128)(2,1)S(1)} %collective-permute-done.6.refs_2_) | copy-start | bytes 6291460
  411.1 17.3 %copy-start.8 = (bf16[2,4,4,32,1024]{4,3,2,1,0:T(8,128)(2,1)}, bf16[2,4,4,32,1024]{4,3,2,1,0:T(8,128)(2,1)S(1)}, u32[]{:S(2)}) copy-start(bf16[2,4,4,32,1024]{4,3,2,1,0:T(8,128)(2,1)S(1)} %collective-permute-done.7.refs_5_.refs_6_) | copy-start | bytes 6291460
  433.7 27.6 %collective-permute-start.8 = (bf16[4,4,32,1024]{3,2,1,0:T(8,128)(2,1)}, bf16[4,4,32,1024]{3,2,1,0:T(8,128)(2,1)S(1)}, u32[]{:S(2)}, u32[]{:S(2)}) collective-permute-start(bf16[4,4,32,1024]{3,2,1,0:T(8,128)(2,1)} %get-tuple-element.196), channel_id=1, source_target_pairs={{0,16},{16,0},{1,17},{17,1},{2,18},{18,2},{3,19},{19,3},{4,20},{20... | collective-permute-start | bytes 3145736 | tf_op jit(solution)/shard_map/ppermute | solution.py:1219
  434.3 27.1 %collective-permute-start.9 = (bf16[4,4,32,1024]{3,2,1,0:T(8,128)(2,1)}, bf16[4,4,32,1024]{3,2,1,0:T(8,128)(2,1)S(1)}, u32[]{:S(2)}, u32[]{:S(2)}) collective-permute-start(bf16[4,4,32,1024]{3,2,1,0:T(8,128)(2,1)} %get-tuple-element.197), channel_id=1, source_target_pairs={{0,2},{1,3},{2,0},{3,1},{4,6},{5,7},{6,4},{7,5},{8,10},{9,11},{10,... | collective-permute-start | bytes 3145736 | tf_op jit(solution)/shard_map/ppermute | solution.py:1223
  461.4 1.0 copy-start.21
  461.4 1.3 copy-start.22
  461.4 7.4 %collective-permute-start.10 = (bf16[2,2,4,2,32,1024]{5,4,3,2,1,0:T(8,128)(2,1)}, bf16[2,2,4,2,32,1024]{5,4,3,2,1,0:T(8,128)(2,1)S(1)}, u32[]{:S(2)}, u32[]{:S(2)}) collective-permute-start(bf16[2,2,4,2,32,1024]{5,4,3,2,1,0:T(8,128)(2,1)} %get-tuple-element.202), channel_id=1, source_target_pairs={{0,1},{1,0},{2,3},{3,2},{4,5},{5,4},{6,7},{7,6},{8,9},{9,8},{10,11... | collective-permute-start | bytes 6291464 | tf_op jit(solution)/shard_map/ppermute | solution.py:1227
  461.5 7.5 %collective-permute-start.11 = (bf16[2,2,4,2,32,1024]{5,4,3,2,1,0:T(8,128)(2,1)}, bf16[2,2,4,2,32,1024]{5,4,3,2,1,0:T(8,128)(2,1)}, u32[]{:S(2)}, u32[]{:S(2)}) collective-permute-start(bf16[2,2,4,2,32,1024]{5,4,3,2,1,0:T(8,128)(2,1)} %get-tuple-element.204), channel_id=1, source_target_pairs={{0,1},{1,0},{2,3},{3,2},{4,5},{5,4},{6,7},{7,6},{8,9},{9,8},{10,11... | collective-permute-start | bytes 6291464 | tf_op jit(solution)/shard_map/ppermute | solution.py:1227
  468.8 1.3 copy-start.3
  475.6 174.1 %reduce-scatter.6.cloned.1.call-start = ((), (), s32[]{:S(2)}) async-start(), calls=%async_computation.4 | async-start | bytes 1638400 | tf_op jit(solution)/shard_map/reduce_scatter | solution.py:1414
  475.6 60.8 %collective-permute-start.12 = (bf16[2,4,5,32,1024]{4,3,2,1,0:T(8,128)(2,1)}, bf16[2,4,5,32,1024]{4,3,2,1,0:T(8,128)(2,1)S(1)}, u32[]{:S(2)}, u32[]{:S(2)}) collective-permute-start(bf16[2,4,5,32,1024]{4,3,2,1,0:T(8,128)(2,1)} %shard_map.260), channel_id=1, source_target_pairs={{0,2},{1,3},{2,0},{3,1},{4,6},{5,7},{6,4},{7,5},{8,10},{9,11},{10,... | collective-permute-start | bytes 7864328 | tf_op jit(solution)/shard_map/ppermute | solution.py:1223
  476.9 59.5 %collective-permute-start.13 = (bf16[768,1024]{1,0:T(8,128)(2,1)}, bf16[768,1024]{1,0:T(8,128)(2,1)}, u32[]{:S(2)}, u32[]{:S(2)}) collective-permute-start(bf16[768,1024]{1,0:T(8,128)(2,1)} %get-tuple-element.211), channel_id=1, source_target_pairs={{0,16},{16,0},{1,17},{17,1},{2,18},{18,2},{3,19},{19,3},{4,20},{20... | collective-permute-start | bytes 4718600 | tf_op jit(solution)/shard_map/ppermute | solution.py:1219
  478.4 57.1 %collective-permute-start.14 = (bf16[512,1024]{1,0:T(8,128)(2,1)}, bf16[512,1024]{1,0:T(8,128)(2,1)S(1)}, u32[]{:S(2)}, u32[]{:S(2)}) collective-permute-start(bf16[512,1024]{1,0:T(8,128)(2,1)} %get-tuple-element.212), channel_id=1, source_target_pairs={{0,16},{16,0},{1,17},{17,1},{2,18},{18,2},{3,19},{19,3},{4,20},{20... | collective-permute-start | bytes 3145736 | tf_op jit(solution)/shard_map/ppermute | solution.py:1219
  535.4 1.0 copy-start.19
  536.4 1.5 copy-start.5
  542.7 18.3 %collective-permute-start.15 = (bf16[4,3,32,1024]{3,2,1,0:T(8,128)(2,1)}, bf16[4,3,32,1024]{3,2,1,0:T(8,128)(2,1)S(1)}, u32[]{:S(2)}, u32[]{:S(2)}) collective-permute-start(bf16[4,3,32,1024]{3,2,1,0:T(8,128)(2,1)} %get-tuple-element.223), channel_id=1, source_target_pairs={{0,16},{16,0},{1,17},{17,1},{2,18},{18,2},{3,19},{19,3},{4,20},{20... | collective-permute-start | bytes 2359304 | tf_op jit(solution)/shard_map/ppermute | solution.py:1219
  561.0 14.7 %copy-start.23 = (bf16[4,3,32,1024]{3,2,1,0:T(8,128)(2,1)}, bf16[4,3,32,1024]{3,2,1,0:T(8,128)(2,1)S(1)}, u32[]{:S(2)}) copy-start(bf16[4,3,32,1024]{3,2,1,0:T(8,128)(2,1)S(1)} %collective-permute-done.15.refs_7_) | copy-start | bytes 2359300
  561.0 5.9 collective-permute-start.17
  561.0 14.7 %collective-permute-start.16 = (bf16[4,2,32,1024]{3,2,1,0:T(8,128)(2,1)}, bf16[4,2,32,1024]{3,2,1,0:T(8,128)(2,1)}, u32[]{:S(2)}, u32[]{:S(2)}) collective-permute-start(bf16[4,2,32,1024]{3,2,1,0:T(8,128)(2,1)} %get-tuple-element.226), channel_id=1, source_target_pairs={{0,16},{16,0},{1,17},{17,1},{2,18},{18,2},{3,19},{19,3},{4,20},{20... | collective-permute-start | bytes 1572872 | tf_op jit(solution)/shard_map/ppermute | solution.py:1219
  566.8 1.7 copy-start.4
  572.5 8.3 %copy-start.17 = (bf16[2,4,3,32,1024]{4,3,2,1,0:T(8,128)(2,1)S(1)}, bf16[2,4,3,32,1024]{4,3,2,1,0:T(8,128)(2,1)}, u32[]{:S(2)}) copy-start(bf16[2,4,3,32,1024]{4,3,2,1,0:T(8,128)(2,1)} %shard_map.265) | copy-start | bytes 4718596
  580.8 83.8 %reduce-scatter.8.cloned.1.call-start = ((), (), s32[]{:S(2)}) async-start(), calls=%async_computation.5 | async-start | bytes 1966080 | tf_op jit(solution)/shard_map/reduce_scatter | solution.py:1414
  580.9 36.1 %collective-permute-start.19 = (bf16[2,4,3,32,1024]{4,3,2,1,0:T(8,128)(2,1)S(1)}, bf16[2,4,3,32,1024]{4,3,2,1,0:T(8,128)(2,1)S(1)}, u32[]{:S(2)}, u32[]{:S(2)}) collective-permute-start(bf16[2,4,3,32,1024]{4,3,2,1,0:T(8,128)(2,1)S(1)} %copy-done.17), channel_id=1, source_target_pairs={{0,2},{1,3},{2,0},{3,1},{4,6},{5,7},{6,4},{7,5},{8,10},{9,11},{10,... | collective-permute-start | bytes 4718600 | tf_op jit(solution)/shard_map/ppermute | solution.py:1223
  581.4 24.5 %collective-permute-start.18 = (bf16[8,32,1024]{2,1,0:T(8,128)(2,1)}, bf16[8,32,1024]{2,1,0:T(8,128)(2,1)}, u32[]{:S(2)}, u32[]{:S(2)}) collective-permute-start(bf16[8,32,1024]{2,1,0:T(8,128)(2,1)} %bitcast.140), channel_id=1, source_target_pairs={{0,16},{16,0},{1,17},{17,1},{2,18},{18,2},{3,19},{19,3},{4,20},{20... | collective-permute-start | bytes 1572872 | tf_op jit(solution)/shard_map/ppermute | solution.py:1219
  604.6 35.8 %collective-permute-start.25 = (bf16[768,1024]{1,0:T(8,128)(2,1)}, bf16[768,1024]{1,0:T(8,128)(2,1)}, u32[]{:S(2)}, u32[]{:S(2)}) collective-permute-start(bf16[768,1024]{1,0:T(8,128)(2,1)} %get-tuple-element.253), channel_id=1, source_target_pairs={{0,16},{16,0},{1,17},{17,1},{2,18},{18,2},{3,19},{19,3},{4,20},{20... | collective-permute-start | bytes 4718600 | tf_op jit(solution)/shard_map/ppermute | solution.py:1219
  617.0 1.1 copy-start.13
  618.1 6.0 copy-start.24
  624.0 20.0 %collective-permute-start.20 = (f32[6,1024]{1,0:T(8,128)S(1)}, f32[6,1024]{1,0:T(8,128)S(1)}, u32[]{:S(2)}, u32[]{:S(2)}) collective-permute-start(f32[6,1024]{1,0:T(8,128)S(1)} %pad_maximum_fusion.6), channel_id=1, source_target_pairs={{0,1},{1,0},{2,3},{3,2},{4,5},{5,4},{6,7},{7,6},{8,9},{9,8},{10,11... | collective-permute-start | bytes 73736 | tf_op jit(solution)/shard_map/ppermute | solution.py:1623
  626.7 1.2 copy-start.18
  626.7 1.5 copy-start.20
  628.3 1.4 copy-start.14
  629.7 10.7 %copy-start.15 = (bf16[768,1024]{1,0:T(8,128)(2,1)S(1)}, bf16[768,1024]{1,0:T(8,128)(2,1)}, u32[]{:S(2)}) copy-start(bf16[768,1024]{1,0:T(8,128)(2,1)} %get-tuple-element.252) | copy-start | bytes 4718596
  644.0 4.0 collective-permute-start.21
  648.0 5.9 collective-permute-start.22
  649.6 14.8 %collective-permute-start.26 = (bf16[5,32,1024]{2,1,0:T(8,128)(2,1)}, bf16[5,32,1024]{2,1,0:T(8,128)(2,1)S(1)}, u32[]{:S(2)}, u32[]{:S(2)}) collective-permute-start(bf16[5,32,1024]{2,1,0:T(8,128)(2,1)} %bitcast.144), channel_id=1, source_target_pairs={{0,16},{16,0},{1,17},{17,1},{2,18},{18,2},{3,19},{19,3},{4,20},{20... | collective-permute-start | bytes 983048 | tf_op jit(solution)/shard_map/ppermute | solution.py:1219
  651.1 4.6 copy-start.10
  651.1 4.6 copy-start.11
  654.0 6.3 collective-permute-start.23
  660.2 4.2 collective-permute-start.24
  661.8 2.7 copy-start.26
  664.6 9.2 %copy-start.25 = (bf16[1,2,3,32,1024]{4,3,2,1,0:T(8,128)(2,1)S(1)}, bf16[1,2,3,32,1024]{4,3,2,1,0:T(8,128)(2,1)}, u32[]{:S(2)}) copy-start(bf16[1,2,3,32,1024]{4,3,2,1,0:T(8,128)(2,1)} %reduce-scatter.8.cloned.1.call-done) | copy-start | bytes 1179652
  665.9 8.0 %collective-permute-start.27 = (bf16[2,3,32,1024]{3,2,1,0:T(8,128)(2,1)}, bf16[2,3,32,1024]{3,2,1,0:T(8,128)(2,1)S(1)}, u32[]{:S(2)}, u32[]{:S(2)}) collective-permute-start(bf16[2,3,32,1024]{3,2,1,0:T(8,128)(2,1)} %bitcast.142), channel_id=1, source_target_pairs={{0,16},{16,0},{1,17},{17,1},{2,18},{18,2},{3,19},{19,3},{4,20},{20... | collective-permute-start | bytes 1179656 | tf_op jit(solution)/shard_map/ppermute | solution.py:1219
  668.5 6.5 copy-start.1
Sparse Core Ops, SparseCore 0:
  12.0 94.2 all-gather.4
  107.8 91.5 all-gather.6
  475.7 43.6 reduce-scatter.3
  580.9 30.3 reduce-scatter.5
  625.4 35.9 reduce-scatter.7
